TPU v7x, 32 devices: a whole 2x2x4 slice. The times are simulated.
32 devices in a mesh: ctx: 8 (over z, x), exp: 4 (over y, core).
Axes of the slice: x: 2, y: 2, z: 4, core: 2. Of those that a mesh axis runs over, the one named last changes fastest.
Arguments:
- queries: bfloat16 [2048, 36864], P('ctx', 'exp'), may hold values from -8 to 8
- latent: bfloat16 [2048, 576], P('ctx'), may hold values from -8 to 8
- block_order: int32 [16], replicated, may hold values from 0 to 15, each once
- w_uv: bfloat16 [64, 512, 128], P('exp'), may hold values from -0.25 to 0.25
- w_o: bfloat16 [8192, 7168], P('exp', 'ctx'), may hold values from -0.0625 to 0.0625
- residual: bfloat16 [2048, 7168], P(('ctx', 'exp')), may hold values from -4 to 4
- norm_gain: bfloat16 [7168], replicated, may hold values from 0.099609375 to 1.8984375
- routes: int32 [2048, 8], P(('ctx', 'exp')), may hold values from 0 to 255, as said below
- route_scores: float32 [2048, 8], P(('ctx', 'exp')), may hold values from 0.05 to 1
- w_gate: bfloat16 [4, 7168, 2048], P('exp', None, 'ctx'), may hold values from -0.0625 to 0.0625
- w_up: bfloat16 [4, 7168, 2048], P('exp', None, 'ctx'), may hold values from -0.0625 to 0.0625
- w_down: bfloat16 [4, 2048, 7168], P('exp', 'ctx'), may hold values from -0.125 to 0.125
Outputs:
- attended: bfloat16 [2048, 7168], P(('ctx', 'exp'))
- expert_part: bfloat16 [2048, 7168], P(('ctx', 'exp'))
Inputs may be any that keep to these rules, and one draw needn't show every extreme that they name: `routes`: each row names 8 different experts; in the rows of one device no expert in flight is named more than 8 times.
All inputs are finite; a program needn't handle non-finite values.
Results may differ from a plain program's by a relative error of at most 0.035.
Values may be sent and summed in bfloat16 or wider, within the bound.
A program may use at most 128 MiB of HBM per device.

v0:
```python
import math

import jax
import jax.numpy as jnp
from jax import lax
from jax.sharding import PartitionSpec as P

EXPERTS = 256
TOP = 8
BLK = 128


def block_places(block_order, rows):
    table = jnp.arange(block_order.shape[0], dtype=jnp.int32)
    pick = (rows // BLK)[:, None] == table[None, :]
    first = jnp.sum(jnp.where(pick, block_order[None, :], 0), axis=1)
    return first * BLK + rows % BLK


def attend(carry, piece, flat_query, query_place, block_order, scale, latent_width):
    length = piece.shape[0]
    part = math.gcd(length, 512)

    def one_part(index, state):
        keys = lax.dynamic_slice_in_dim(piece, index * part, part, 0)
        offset = index * part + jnp.arange(part, dtype=jnp.int32)
        allowed = block_places(block_order, offset)[None, :] <= query_place[:, None]

        def update(inner):
            highest, total, weighted = inner
            scores = (
                lax.dot_general(
                    flat_query, keys, (((1,), (1,)), ((), ())), preferred_element_type=jnp.float32
                )
                * scale
            )
            scores = jnp.where(allowed, scores, -1e30)
            newest = jnp.maximum(highest, jnp.max(scores, axis=1))
            shrink = jnp.exp(highest - newest)
            weights = jnp.where(allowed, jnp.exp(scores - newest[:, None]), 0.0)
            total = total * shrink + jnp.sum(weights, axis=1)
            weighted = weighted * shrink[:, None] + jnp.dot(
                weights.astype(jnp.bfloat16),
                keys[:, :latent_width],
                preferred_element_type=jnp.float32,
            )
            return (newest, total, weighted)

        return lax.cond(jnp.any(allowed), update, lambda inner: inner, state)

    return lax.fori_loop(0, length // part, one_part, carry)


def per_device(
    queries,
    latent,
    block_order,
    w_uv,
    w_o,
    residual,
    norm_gain,
    routes,
    route_scores,
    w_gate,
    w_up,
    w_down,
):
    owner_count = lax.axis_size("exp")
    seq_block = queries.shape[0]
    head_count, latent_width, value_width = w_uv.shape
    key_width = latent.shape[1]
    token_count = residual.shape[0]
    model_width = residual.shape[1]
    scale = (value_width + key_width - latent_width) ** (-0.5)
    rows_here = lax.axis_index("ctx") * seq_block + jnp.arange(seq_block, dtype=jnp.int32)
    query_place = jnp.repeat(block_places(block_order, rows_here), head_count)
    flat_query = queries.reshape(seq_block * head_count, key_width)
    query_rows = seq_block * head_count
    start_state = (
        jnp.full((query_rows,), -1e30, jnp.float32),
        jnp.zeros((query_rows,), jnp.float32),
        jnp.zeros((query_rows, latent_width), jnp.float32),
    )
    highest, total, weighted = attend(
        start_state,
        lax.all_gather(latent, "ctx", axis=0, tiled=True),
        flat_query,
        query_place,
        block_order,
        scale,
        latent_width,
    )
    attn_latent = (
        (weighted / total[:, None])
        .astype(jnp.bfloat16)
        .reshape(seq_block, head_count, latent_width)
    )
    heads = jnp.einsum(
        "thl,hlv->thv", attn_latent, w_uv, preferred_element_type=jnp.float32
    ).astype(jnp.bfloat16)
    heads = heads.reshape(seq_block, head_count * value_width)
    full_columns = lax.all_gather(w_o, "ctx", axis=1, tiled=True)
    projected = lax.psum_scatter(
        jnp.dot(heads, full_columns, preferred_element_type=jnp.float32).astype(jnp.bfloat16),
        "exp",
        scatter_dimension=0,
        tiled=True,
    ).astype(jnp.float32)
    attended = (residual.astype(jnp.float32) + projected).astype(jnp.bfloat16)
    level = attended.astype(jnp.float32)
    normed = (
        level
        * lax.rsqrt(jnp.mean(level * level, axis=1, keepdims=True) + 1e-06)
        * norm_gain.astype(jnp.float32)
    ).astype(jnp.bfloat16)
    share = 2.5 * route_scores / jnp.sum(route_scores, axis=1, keepdims=True)
    per_owner = EXPERTS // owner_count
    chosen = jnp.arange(owner_count, dtype=jnp.int32) * per_owner
    match = routes[:, :, None] == chosen[None, None, :]
    hits = jnp.sum(match.astype(jnp.int32), axis=1)
    weight_to = jnp.sum(jnp.where(match, share[:, :, None], 0.0), axis=1)
    ranking = jnp.cumsum(hits, axis=0) - 1
    capacity = max(2, 4 * token_count * TOP // EXPERTS)
    slot_ids = jnp.arange(capacity, dtype=jnp.int32)
    select = ((hits[:, :, None] == 1) & (ranking[:, :, None] == slot_ids[None, None, :])).astype(
        jnp.bfloat16
    )
    outgoing = jnp.einsum("toc,td->ocd", select, normed, preferred_element_type=jnp.float32).astype(
        jnp.bfloat16
    )
    arrived = lax.all_to_all(outgoing, "exp", split_axis=0, concat_axis=0, tiled=True)
    flat_rows = arrived.reshape(owner_count * capacity, model_width)
    piece = lax.all_gather(flat_rows, "ctx", axis=0, tiled=True)
    gate = jnp.dot(piece, w_gate[0], preferred_element_type=jnp.float32)
    lifted = jnp.dot(piece, w_up[0], preferred_element_type=jnp.float32)
    hidden = (jax.nn.silu(gate) * lifted).astype(jnp.bfloat16)
    lowered = lax.psum_scatter(
        jnp.dot(hidden, w_down[0], preferred_element_type=jnp.float32).astype(jnp.bfloat16),
        "ctx",
        scatter_dimension=0,
        tiled=True,
    )
    expert_out = lowered.reshape(owner_count, capacity, model_width)
    returned = lax.all_to_all(expert_out, "exp", split_axis=0, concat_axis=0, tiled=True)
    picked = jnp.einsum("toc,ocd->otd", select, returned, preferred_element_type=jnp.float32)
    expert_part = jnp.sum(picked * jnp.transpose(weight_to)[:, :, None], axis=0).astype(
        jnp.bfloat16
    )
    return (attended, expert_part)


def solution(mesh):
    return jax.shard_map(
        per_device,
        mesh=mesh,
        in_specs=(
            P("ctx", "exp"),
            P("ctx", None),
            P(),
            P("exp", None, None),
            P("exp", "ctx"),
            P(("ctx", "exp"), None),
            P(),
            P(("ctx", "exp"), None),
            P(("ctx", "exp"), None),
            P("exp", None, "ctx"),
            P("exp", None, "ctx"),
            P("exp", "ctx", None),
        ),
        out_specs=(P(("ctx", "exp"), None), P(("ctx", "exp"), None)),
        check_vma=False,
    )
```

profile of v0, /device:TPU:0, one launch (start us, length us, event | category | flops | bytes accessed | tf_op | source)
XLA Modules:
  0.0 878.6 jit_solution(4506800252399846029)
XLA Ops:
  10.1 8.9 %reshape.108 = bf16[4096,576]{1,0:T(8,128)(2,1)} reshape(bf16[256,9216]{1,0:T(8,128)(2,1)} %param.16) | data formatting | bytes 9437184 | tf_op jit(solution)/shard_map/reshape | solution.py:77
  19.1 49.1 %all-gather.4.cloned.1.call-done = bf16[2048,576]{1,0:T(8,128)(2,1)} async-done(((bf16[256,576]{1,0:T(8,128)(2,1)}), bf16[2048,576]{1,0:T(8,128)(2,1)}) %all-gather.4.cloned.1.call-update) | async-done | bytes 2359312 | tf_op jit(solution)/shard_map/all_gather | solution.py:86
  68.2 4.4 broadcast_in_dim.105
  72.6 79.3 %while.20 = (s32[]{:T(128)}, f32[4096]{0:T(1024)S(1)}, f32[4096]{0:T(1024)S(1)}, f32[4096,512]{1,0:T(8,128)}, s32[16]{0:T(128)S(1)}, /*index=5*/bf16[2048,576]{1...) while((s32[]{:T(128)}, f32[4096]{0:T(1024)S(1)}, ...), condition=%wide.region_8.9_spmd.clone, body=%wide.region_1.8_spmd.clone.sunk | while | flops 4599101952 | bytes 132593072 | solution.py:51
  72.9 3.7 broadcast_compare_fusion.4
  77.3 20.2 %conditional.3 = ((f32[4096]{0:T(1024)S(1)}, f32[4096]{0:T(1024)S(1)}, f32[4096,512]{1,0:T(8,128)})) conditional(s32[]{:T(128)} %convert_element_type.111, (f32[4096]{0:T(1024)S(1)}, f32[4096]{0:T(1024)S(1)}, f32[4096,512]{1,0:T(8,128)}) %tuple.65, (s32[]{:T(128)}, bf16[2048,576]{1,0:T(8,128)(2,1)}, bf16[4096,576]{1,0:T(8,128)(2,1)}, ...), branch_computations={%region_4.4_spmd, %region_5.7_spmd} | conditional | flops 4594868224 | bytes 130416792 | solution.py:49
  77.3 7.5 fusion.2
  88.2 6.0 multiply_add_fusion
  94.2 3.3 copy-done.3
  97.9 3.7 broadcast_compare_fusion.4
  102.6 3.7 broadcast_compare_fusion.4
  107.0 20.0 %conditional.3 = ((f32[4096]{0:T(1024)S(1)}, f32[4096]{0:T(1024)S(1)}, f32[4096,512]{1,0:T(8,128)})) conditional(s32[]{:T(128)} %convert_element_type.111, (f32[4096]{0:T(1024)S(1)}, f32[4096]{0:T(1024)S(1)}, f32[4096,512]{1,0:T(8,128)}) %tuple.65, (s32[]{:T(128)}, bf16[2048,576]{1,0:T(8,128)(2,1)}, bf16[4096,576]{1,0:T(8,128)(2,1)}, ...), branch_computations={%region_4.4_spmd, %region_5.7_spmd} | conditional | flops 4594868224 | bytes 130416792 | solution.py:49
  107.1 7.3 fusion.2
  117.7 6.0 multiply_add_fusion
  123.7 3.3 copy-done.3
  127.4 3.7 broadcast_compare_fusion.4
  131.8 20.1 %conditional.3 = ((f32[4096]{0:T(1024)S(1)}, f32[4096]{0:T(1024)S(1)}, f32[4096,512]{1,0:T(8,128)})) conditional(s32[]{:T(128)} %convert_element_type.111, (f32[4096]{0:T(1024)S(1)}, f32[4096]{0:T(1024)S(1)}, f32[4096,512]{1,0:T(8,128)}) %tuple.65, (s32[]{:T(128)}, bf16[2048,576]{1,0:T(8,128)(2,1)}, bf16[4096,576]{1,0:T(8,128)(2,1)}, ...), branch_computations={%region_4.4_spmd, %region_5.7_spmd} | conditional | flops 4594868224 | bytes 130416792 | solution.py:49
  131.8 7.3 fusion.2
  142.6 6.0 multiply_add_fusion
  148.5 3.3 copy-done.3
  151.9 4.2 divide_convert_fusion
  156.1 2.7 fusion.34
  158.8 468.7 %all-gather.6.cloned.1.call-done = bf16[2048,7168]{1,0:T(8,128)(2,1)} async-done(((bf16[2048,896]{1,0:T(8,128)(2,1)}), bf16[2048,7168]{1,0:T(8,128)(2,1)}) %all-gather.6.cloned.1.call-update) | async-done | bytes 29360144 | tf_op jit(solution)/shard_map/all_gather | solution.py:102
  627.4 14.6 %convolution_convert_fusion.1 = bf16[256,7168]{1,0:T(8,128)(2,1)} fusion(bf16[256,2048]{0,1:T(8,128)(2,1)S(1)} %bitcast.45, bf16[2048,7168]{1,0:T(8,128)(2,1)} %all-gather.6.cloned.1.call-done), kind=kOutput, calls=%fused_computation.38 | convolution fusion | flops 7518027776 | bytes 34078720 | tf_op jit(solution)/shard_map/dot_general | solution.py:104
  642.6 40.9 %reduce-scatter.3.cloned.1.call-done = bf16[64,7168]{1,0:T(8,128)(2,1)} async-done(((bf16[256,7168]{1,0:T(8,128)(2,1)}), bf16[64,7168]{1,0:T(8,128)(2,1)}) %reduce-scatter.3.cloned.1.call-update) | async-done | bytes 917520 | tf_op jit(solution)/shard_map/reduce_scatter | solution.py:103
  686.5 11.2 %all_to_all.10 = bf16[4,8,7168]{2,1,0:T(8,128)(2,1)} all-to-all(bf16[4,8,7168]{2,1,0:T(8,128)(2,1)S(1)} %convolution_convert_fusion.2), channel_id=1, replica_groups=mesh['ctx'=8,'exp'=4] {'exp'}, dimensions={0} | all-to-all | bytes 917504 | tf_op jit(solution)/shard_map/all_to_all | solution.py:131
  697.8 66.9 %all-gather.8.cloned.1.call-done = bf16[256,7168]{1,0:T(8,128)(2,1)} async-done(((bf16[32,7168]{1,0:T(8,128)(2,1)}), bf16[256,7168]{1,0:T(8,128)(2,1)}) %all-gather.8.cloned.1.call-update) | async-done | bytes 3670032 | tf_op jit(solution)/shard_map/all_gather | solution.py:133
  764.7 4.3 fusion.28
  768.9 10.0 %convolution_convert_fusion = bf16[256,7168]{1,0:T(8,128)(2,1)} fusion(bf16[1,256,7168]{2,1,0:T(8,128)(2,1)} %param.27, bf16[256,7168]{1,0:T(8,128)(2,1)} %all-gather.8.cloned.1.call-done, bf16[1,7168,256]{2,1,0:T(8,128)(2,1)} %param.26, f32[256,256]{1,0:T(8,128)S(1)} %fusion.28), kind=kOutput, calls=%fused_computation.37 | convolution fusion | flops 1881276416 | bytes 14942208 | tf_op jit(solution)/shard_map/dot_general | solution.py:138
  779.0 79.3 %reduce-scatter.5.cloned.1.call-done = bf16[32,7168]{1,0:T(8,128)(2,1)} async-done(((bf16[256,7168]{1,0:T(8,128)(2,1)}), bf16[32,7168]{1,0:T(8,128)(2,1)}) %reduce-scatter.5.cloned.1.call-update) | async-done | bytes 458768 | tf_op jit(solution)/shard_map/reduce_scatter | solution.py:137
  858.4 3.5 all-to-all-start.1
  862.0 8.0 all-to-all-done.1
  (93 shorter events, 20.0 us)
Async XLA Ops:
  7.2 148.9 %copy-start = (bf16[16,512,128]{2,1,0:T(8,128)(2,1)S(1)}, bf16[16,512,128]{2,1,0:T(8,128)(2,1)}, u32[]{:S(2)}) copy-start(bf16[16,512,128]{2,1,0:T(8,128)(2,1)} %param.19) | copy-start | bytes 6291460
  7.2 61.0 %all-gather.4.cloned.1.call-start = ((), (), s32[]{:S(2)}) async-start(), calls=%async_computation.4 | async-start | bytes 2949120 | tf_op jit(solution)/shard_map/all_gather | solution.py:86
  9.2 618.2 %all-gather.6.cloned.1.call-start = ((), (), s32[]{:S(2)}) async-start(), calls=%async_computation.5 | async-start | bytes 33030144 | tf_op jit(solution)/shard_map/all_gather | solution.py:102
  10.0 673.5 %reduce-scatter.3.cloned.1.call-start = ((), (), s32[]{:S(2)}) async-start(), calls=%async_computation.6 | async-start | bytes 4587520 | tf_op jit(solution)/shard_map/reduce_scatter | solution.py:103
  10.0 8.9 %copy-start.6 = (s32[16]{0:T(128)S(1)}, s32[16]{0:T(128)}, u32[]{:S(2)}) copy-start(s32[16]{0:T(128)} %param.18) | copy-start | bytes 196
  77.3 7.5 copy-start.1
  84.8 3.4 copy-start.2
  94.2 3.3 copy-start.3
  107.1 7.3 copy-start.1
  114.4 3.4 copy-start.2
  123.7 3.3 copy-start.3
  131.8 7.4 copy-start.1
  139.2 3.4 copy-start.2
  148.5 3.3 copy-start.3
  627.4 14.7 %copy-start.9 = (bf16[7168]{0:T(1024)(128)(2,1)S(1)}, bf16[7168]{0:T(1024)(128)(2,1)}, u32[]{:S(2)}) copy-start(bf16[7168]{0:T(1024)(128)(2,1)} %param.22) | copy-start | bytes 43012
  627.4 14.8 %copy-start.8 = (s32[64,8]{0,1:T(8,128)S(1)}, s32[64,8]{0,1:T(8,128)}, u32[]{:S(2)}) copy-start(s32[64,8]{0,1:T(8,128)} %param.23) | copy-start | bytes 6148
  642.1 41.4 %copy-start.4 = (bf16[64,7168]{1,0:T(8,128)(2,1)S(1)}, bf16[64,7168]{1,0:T(8,128)(2,1)}, u32[]{:S(2)}) copy-start(bf16[64,7168]{1,0:T(8,128)(2,1)} %param.21) | copy-start | bytes 2752516
  642.1 122.6 %all-gather.8.cloned.1.call-start = ((), (), s32[]{:S(2)}) async-start(), calls=%async_computation.7 | async-start | bytes 4128768 | tf_op jit(solution)/shard_map/all_gather | solution.py:133
  685.1 0.9 copy-start.5
  697.7 160.6 %reduce-scatter.5.cloned.1.call-start = ((), (), s32[]{:S(2)}) async-start(), calls=%async_computation.8 | async-start | bytes 4128768 | tf_op jit(solution)/shard_map/reduce_scatter | solution.py:137
  779.0 82.8 %copy-start.7 = (f32[64,8]{0,1:T(8,128)S(1)}, f32[64,8]{0,1:T(8,128)}, u32[]{:S(2)}) copy-start(f32[64,8]{0,1:T(8,128)} %param.24) | copy-start | bytes 6148
  858.4 11.6 %all-to-all-start.1 = ((bf16[4,8,7168]{2,1,0:T(8,128)(2,1)}), bf16[4,8,7168]{2,1,0:T(8,128)(2,1)S(1)}, u32[]{:S(2)}, u32[]{:S(2)}) async-start(bf16[4,8,7168]{2,1,0:T(8,128)(2,1)} %bitcast.46), calls=%async_computation.3 | async-start | bytes 917504 | tf_op jit(solution)/shard_map/all_to_all | solution.py:144
Sparse Core Ops, SparseCore 0:
  10.8 57.3 all-gather.3
  69.7 557.6 all-gather.5
  642.2 41.2 reduce-scatter.2
  697.8 66.7 all-gather.7
  779.1 79.1 reduce-scatter.4
where the time goes:
time: 879 us
  waiting for transfers between devices  714 us (81%)
  matrix products  74.2 us (8%)
  local copies, waits for them, and re-layouts  29.5 us (3%)
  other arithmetic  29.3 us (3%)
  between operations  13.9 us (2%)
  blocking collectives  11.2 us (1%)
    all_gather x1, waiting for transfers between devices, per_device(): full_columns = lax.all_gather(w_o, 'ctx', axis=1, tiled=True)  469 us
    reduce_scatter x1, waiting for transfers between devices, per_device(): lax.psum_scatter(jnp.dot(hidden, w_down[0], preferred_element_type=jnp.fl...  79.3 us
    all_gather x1, waiting for transfers between devices, per_device(): piece = lax.all_gather(flat_rows, 'ctx', axis=0, tiled=True)  66.9 us
    all_gather x1, waiting for transfers between devices, per_device(): lax.all_gather(latent, 'ctx', axis=0, tiled=True)  49.1 us
    reduce_scatter x1, waiting for transfers between devices, per_device(): lax.psum_scatter(jnp.dot(heads, full_columns, preferred_element_type=jnp....  40.9 us
    dot_general x3, matrix products, update(): lax.dot_general(flat_query, keys, (((1,), (1,)), ((), ())), preferred_ele...  22.1 us
    dot_general x3, matrix products, update(): jnp.dot(weights.astype(jnp.bfloat16), keys[:, :latent_width], preferred_e...  17.9 us
  transfers between devices with their start and end apart: 6, of which 6 were waited for; matrix products, arithmetic and copies ran while one was open for 10% of the time, Pallas kernels for 0%

commit v1 on v0

--- a/solution.py
+++ b/solution.py
@@ -8,6 +8,7 @@
 EXPERTS = 256
 TOP = 8
 BLK = 128
+PAIR = 2
 
 
 def block_places(block_order, rows):
@@ -99,13 +100,32 @@
         "thl,hlv->thv", attn_latent, w_uv, preferred_element_type=jnp.float32
     ).astype(jnp.bfloat16)
     heads = heads.reshape(seq_block, head_count * value_width)
-    full_columns = lax.all_gather(w_o, "ctx", axis=1, tiled=True)
-    projected = lax.psum_scatter(
-        jnp.dot(heads, full_columns, preferred_element_type=jnp.float32).astype(jnp.bfloat16),
+    ctx_count = lax.axis_size("ctx")
+    levels = ctx_count // PAIR
+    other = lax.ppermute(w_o, "ctx", [(c, c ^ 1) for c in range(ctx_count)])
+    first = lax.axis_index("ctx") % PAIR == 0
+    pair_columns = jnp.concatenate(
+        [jnp.where(first, w_o, other), jnp.where(first, other, w_o)], axis=1
+    )
+    lines = [[level * PAIR + side for level in range(levels)] for side in range(PAIR)]
+    line_heads = lax.all_gather(heads, "ctx", axis=0, tiled=True, axis_index_groups=lines)
+    terms = jnp.dot(line_heads, pair_columns, preferred_element_type=jnp.float32).astype(
+        jnp.bfloat16
+    )
+    width = terms.shape[1]
+    terms = jnp.swapaxes(terms.reshape(levels, owner_count, token_count, width), 0, 1)
+    summed = lax.psum_scatter(
+        terms.reshape(owner_count * levels * token_count, width),
         "exp",
         scatter_dimension=0,
         tiled=True,
-    ).astype(jnp.float32)
+    ).reshape(levels, token_count, width)
+    spread = lax.all_to_all(
+        summed, "ctx", split_axis=0, concat_axis=0, tiled=True, axis_index_groups=lines
+    )
+    projected = (
+        jnp.swapaxes(spread, 0, 1).reshape(token_count, model_width).astype(jnp.float32)
+    )
     attended = (residual.astype(jnp.float32) + projected).astype(jnp.bfloat16)
     level = attended.astype(jnp.float32)
     normed = (

time: 879 us -> 542 us (0.62)
  waiting for transfers between devices: 714 us -> 345 us
  matrix products: 74.2 us -> 85.4 us
    all_gather x1, waiting for transfers between devices: 469 us -> 0.01 us  [per_device(): lax.all_gather(heads, 'ctx', axis=0, tiled=True, axis_index_groups=lines)]
    ppermute x0 -> x1, waiting for transfers between devices: none -> 79.6 us  [per_device(): other = lax.ppermute(w_o, 'ctx', [(c, c ^ 1) for c in range(ctx_count)])]
    all_to_all x0 -> x1, waiting for transfers between devices: none -> 22.5 us  [per_device(): lax.all_to_all(summed, 'ctx', split_axis=0, concat_axis=0, tiled=True, ax...]
    dot_general x3 -> x4, matrix products: 22.1 us -> 29.1 us  [update(): lax.dot_general(flat_query, keys, (((1,), (1,)), ((), ())), preferred_ele...]
    dot_general x3 -> x4, matrix products: 17.9 us -> 23.8 us  [update(): jnp.dot(weights.astype(jnp.bfloat16), keys[:, :latent_width], preferred_e...]
  transfers between devices with their start and end apart: 6 -> 8, of which waited for: 6 -> 7; matrix products, arithmetic and copies ran while one was open for 10% -> 3% of each run, Pallas kernels for 0% -> 0%
where the time goes in v1:
time: 542 us; the launch traced here: 541 us
  waiting for transfers between devices  345 us (64%)
  matrix products  85.4 us (16%)
  other arithmetic  37.4 us (7%)
  local copies, waits for them, and re-layouts  35.3 us (7%)
  between operations  13.9 us (3%)
  blocking collectives  11.2 us (2%)
  starting transfers between devices  9.07 us (2%)
    ppermute x1, waiting for transfers between devices, per_device(): other = lax.ppermute(w_o, 'ctx', [(c, c ^ 1) for c in range(ctx_count)])  79.6 us
    reduce_scatter x1, waiting for transfers between devices, per_device(): lax.psum_scatter(jnp.dot(hidden, w_down[0], preferred_element_type=jnp.fl...  79.5 us
    all_gather x1, waiting for transfers between devices, per_device(): piece = lax.all_gather(flat_rows, 'ctx', axis=0, tiled=True)  64.8 us
    all_gather x1, waiting for transfers between devices, per_device(): lax.all_gather(latent, 'ctx', axis=0, tiled=True)  49.8 us
    reduce_scatter x1, waiting for transfers between devices, per_device(): lax.psum_scatter(terms.reshape(owner_count * levels * token_count, width)...  41.2 us
    dot_general x4, matrix products, update(): lax.dot_general(flat_query, keys, (((1,), (1,)), ((), ())), preferred_ele...  29.1 us
    dot_general x4, matrix products, update(): jnp.dot(weights.astype(jnp.bfloat16), keys[:, :latent_width], preferred_e...  23.8 us
    all_to_all x1, waiting for transfers between devices, per_device(): lax.all_to_all(summed, 'ctx', split_axis=0, concat_axis=0, tiled=True, ax...  22.5 us
  transfers between devices with their start and end apart: 8, of which 7 were waited for; matrix products, arithmetic and copies ran while one was open for 3% of the time, Pallas kernels for 0%

profile of v1, /device:TPU:0, one launch (start us, length us, event | category | flops | bytes accessed | tf_op | source)
XLA Modules:
  0.0 540.8 jit_solution(5110479467774980204)
XLA Ops:
  9.3 9.0 %reshape.120 = bf16[4096,576]{1,0:T(8,128)(2,1)} reshape(bf16[256,9216]{1,0:T(8,128)(2,1)} %param.16) | data formatting | bytes 9437184 | tf_op jit(solution)/shard_map/reshape | solution.py:78
  18.4 49.8 %all-gather.4.cloned.1.call-done = bf16[2048,576]{1,0:T(8,128)(2,1)} async-done(((bf16[256,576]{1,0:T(8,128)(2,1)}), bf16[2048,576]{1,0:T(8,128)(2,1)}) %all-gather.4.cloned.1.call-update) | async-done | bytes 2359312 | tf_op jit(solution)/shard_map/all_gather | solution.py:87
  68.2 4.3 broadcast_in_dim.105
  72.5 98.3 %while.20 = (s32[]{:T(128)}, f32[4096]{0:T(1024)S(1)}, f32[4096]{0:T(1024)S(1)}, f32[4096,512]{1,0:T(8,128)}, s32[16]{0:T(128)S(1)}, /*index=5*/bf16[2048,576]{1...) while((s32[]{:T(128)}, f32[4096]{0:T(1024)S(1)}, ...), condition=%wide.region_8.9_spmd.clone, body=%wide.region_1.8_spmd.clone.sunk | while | flops 4599101952 | bytes 132593072 | solution.py:52
  72.8 3.7 broadcast_compare_fusion.4
  77.2 19.9 %conditional.3 = ((f32[4096]{0:T(1024)S(1)}, f32[4096]{0:T(1024)S(1)}, f32[4096,512]{1,0:T(8,128)})) conditional(s32[]{:T(128)} %convert_element_type.120, (f32[4096]{0:T(1024)S(1)}, f32[4096]{0:T(1024)S(1)}, f32[4096,512]{1,0:T(8,128)}) %tuple.66, (s32[]{:T(128)}, bf16[2048,576]{1,0:T(8,128)(2,1)}, bf16[4096,576]{1,0:T(8,128)(2,1)}, ...), branch_computations={%region_4.4_spmd, %region_5.7_spmd} | conditional | flops 4594868224 | bytes 130416792 | solution.py:50
  77.2 7.3 %fusion.2 = (f32[4096]{0:T(1024)S(1)}, f32[512,4096]{1,0:T(8,128)S(1)}) fusion(pred[4096,512]{0,1:T(32,128)(4,1)} %get-tuple-element.257, bf16[4096,576]{1,0:T(8,128)(2,1)} %get-tuple-element.260, bf16[2048,576]{1,0:T(8,128)(2,1)} %get-tuple-element.258, s32[]{:T(128)S(6)} %select_n.97), kind=kOutput, calls=%fused_computation.4 | convolution fusion | flops 2422206464 | bytes 16400388 | tf_op jit(solution)/shard_map/while/body/eval_jaxpr/cond/branch_1_fun/dot_general | solution.py:33
  87.9 6.0 %multiply_add_fusion = f32[4096,512]{1,0:T(8,128)S(1)} fusion(f32[4096,512]{1,0:T(8,128)S(1)} %copy-done.2, pred[4096,512]{0,1:T(32,128)(4,1)S(1)} %copy-done.1, f32[512,4096]{1,0:T(8,128)S(1)} %get-tuple-element.324, f32[4096]{0:T(1024)S(1)} %get-tuple-element.320, f32[4096]{0:T(1024)S(1)} %max.3, bf16[2048,576]{1,0:T(8,128)(2,1)} %get-tuple-element.258, ...), kind=kOutput, calls=%fused_computation.2 | convolution fusion | flops 2162163712 | bytes 27820036 | tf_op jit(solution)/shard_map/while/body/eval_jaxpr/cond/branch_1_fun/dot_general | solution.py:43
  97.4 3.7 broadcast_compare_fusion.4
  101.7 19.9 %conditional.3 = ((f32[4096]{0:T(1024)S(1)}, f32[4096]{0:T(1024)S(1)}, f32[4096,512]{1,0:T(8,128)})) conditional(s32[]{:T(128)} %convert_element_type.120, (f32[4096]{0:T(1024)S(1)}, f32[4096]{0:T(1024)S(1)}, f32[4096,512]{1,0:T(8,128)}) %tuple.66, (s32[]{:T(128)}, bf16[2048,576]{1,0:T(8,128)(2,1)}, bf16[4096,576]{1,0:T(8,128)(2,1)}, ...), branch_computations={%region_4.4_spmd, %region_5.7_spmd} | conditional | flops 4594868224 | bytes 130416792 | solution.py:50
  101.8 7.3 %fusion.2 = (f32[4096]{0:T(1024)S(1)}, f32[512,4096]{1,0:T(8,128)S(1)}) fusion(pred[4096,512]{0,1:T(32,128)(4,1)} %get-tuple-element.257, bf16[4096,576]{1,0:T(8,128)(2,1)} %get-tuple-element.260, bf16[2048,576]{1,0:T(8,128)(2,1)} %get-tuple-element.258, s32[]{:T(128)S(6)} %select_n.97), kind=kOutput, calls=%fused_computation.4 | convolution fusion | flops 2422206464 | bytes 16400388 | tf_op jit(solution)/shard_map/while/body/eval_jaxpr/cond/branch_1_fun/dot_general | solution.py:33
  112.5 6.0 %multiply_add_fusion = f32[4096,512]{1,0:T(8,128)S(1)} fusion(f32[4096,512]{1,0:T(8,128)S(1)} %copy-done.2, pred[4096,512]{0,1:T(32,128)(4,1)S(1)} %copy-done.1, f32[512,4096]{1,0:T(8,128)S(1)} %get-tuple-element.324, f32[4096]{0:T(1024)S(1)} %get-tuple-element.320, f32[4096]{0:T(1024)S(1)} %max.3, bf16[2048,576]{1,0:T(8,128)(2,1)} %get-tuple-element.258, ...), kind=kOutput, calls=%fused_computation.2 | convolution fusion | flops 2162163712 | bytes 27820036 | tf_op jit(solution)/shard_map/while/body/eval_jaxpr/cond/branch_1_fun/dot_general | solution.py:43
  126.3 19.9 %conditional.3 = ((f32[4096]{0:T(1024)S(1)}, f32[4096]{0:T(1024)S(1)}, f32[4096,512]{1,0:T(8,128)})) conditional(s32[]{:T(128)} %convert_element_type.120, (f32[4096]{0:T(1024)S(1)}, f32[4096]{0:T(1024)S(1)}, f32[4096,512]{1,0:T(8,128)}) %tuple.66, (s32[]{:T(128)}, bf16[2048,576]{1,0:T(8,128)(2,1)}, bf16[4096,576]{1,0:T(8,128)(2,1)}, ...), branch_computations={%region_4.4_spmd, %region_5.7_spmd} | conditional | flops 4594868224 | bytes 130416792 | solution.py:50
  126.4 7.3 %fusion.2 = (f32[4096]{0:T(1024)S(1)}, f32[512,4096]{1,0:T(8,128)S(1)}) fusion(pred[4096,512]{0,1:T(32,128)(4,1)} %get-tuple-element.257, bf16[4096,576]{1,0:T(8,128)(2,1)} %get-tuple-element.260, bf16[2048,576]{1,0:T(8,128)(2,1)} %get-tuple-element.258, s32[]{:T(128)S(6)} %select_n.97), kind=kOutput, calls=%fused_computation.4 | convolution fusion | flops 2422206464 | bytes 16400388 | tf_op jit(solution)/shard_map/while/body/eval_jaxpr/cond/branch_1_fun/dot_general | solution.py:33
  137.0 6.0 %multiply_add_fusion = f32[4096,512]{1,0:T(8,128)S(1)} fusion(f32[4096,512]{1,0:T(8,128)S(1)} %copy-done.2, pred[4096,512]{0,1:T(32,128)(4,1)S(1)} %copy-done.1, f32[512,4096]{1,0:T(8,128)S(1)} %get-tuple-element.324, f32[4096]{0:T(1024)S(1)} %get-tuple-element.320, f32[4096]{0:T(1024)S(1)} %max.3, bf16[2048,576]{1,0:T(8,128)(2,1)} %get-tuple-element.258, ...), kind=kOutput, calls=%fused_computation.2 | convolution fusion | flops 2162163712 | bytes 27820036 | tf_op jit(solution)/shard_map/while/body/eval_jaxpr/cond/branch_1_fun/dot_general | solution.py:43
  150.9 19.9 %conditional.3 = ((f32[4096]{0:T(1024)S(1)}, f32[4096]{0:T(1024)S(1)}, f32[4096,512]{1,0:T(8,128)})) conditional(s32[]{:T(128)} %convert_element_type.120, (f32[4096]{0:T(1024)S(1)}, f32[4096]{0:T(1024)S(1)}, f32[4096,512]{1,0:T(8,128)}) %tuple.66, (s32[]{:T(128)}, bf16[2048,576]{1,0:T(8,128)(2,1)}, bf16[4096,576]{1,0:T(8,128)(2,1)}, ...), branch_computations={%region_4.4_spmd, %region_5.7_spmd} | conditional | flops 4594868224 | bytes 130416792 | solution.py:50
  150.9 7.3 %fusion.2 = (f32[4096]{0:T(1024)S(1)}, f32[512,4096]{1,0:T(8,128)S(1)}) fusion(pred[4096,512]{0,1:T(32,128)(4,1)} %get-tuple-element.257, bf16[4096,576]{1,0:T(8,128)(2,1)} %get-tuple-element.260, bf16[2048,576]{1,0:T(8,128)(2,1)} %get-tuple-element.258, s32[]{:T(128)S(6)} %select_n.97), kind=kOutput, calls=%fused_computation.4 | convolution fusion | flops 2422206464 | bytes 16400388 | tf_op jit(solution)/shard_map/while/body/eval_jaxpr/cond/branch_1_fun/dot_general | solution.py:33
  161.6 6.0 %multiply_add_fusion = f32[4096,512]{1,0:T(8,128)S(1)} fusion(f32[4096,512]{1,0:T(8,128)S(1)} %copy-done.2, pred[4096,512]{0,1:T(32,128)(4,1)S(1)} %copy-done.1, f32[512,4096]{1,0:T(8,128)S(1)} %get-tuple-element.324, f32[4096]{0:T(1024)S(1)} %get-tuple-element.320, f32[4096]{0:T(1024)S(1)} %max.3, bf16[2048,576]{1,0:T(8,128)(2,1)} %get-tuple-element.258, ...), kind=kOutput, calls=%fused_computation.2 | convolution fusion | flops 2162163712 | bytes 27820036 | tf_op jit(solution)/shard_map/while/body/eval_jaxpr/cond/branch_1_fun/dot_general | solution.py:43
  170.8 4.0 divide_convert_fusion
  174.8 3.7 fusion.41
  179.3 79.6 %collective-permute-done = bf16[2048,896]{1,0:T(8,128)(2,1)} collective-permute-done((bf16[2048,896]{1,0:T(8,128)(2,1)}, bf16[2048,896]{1,0:T(8,128)(2,1)}, u32[]{:S(2)}, u32[]{:S(2)}) %collective-permute-start) | collective-permute-done | bytes 3670048 | tf_op jit(solution)/shard_map/ppermute | solution.py:105
  258.8 6.9 %broadcast_select_fusion.1 = (bf16[2048,896]{1,0:T(8,128)(2,1)}, bf16[2048,896]{1,0:T(8,128)(2,1)}) fusion(bf16[2048,896]{1,0:T(8,128)(2,1)} %param.20, bf16[2048,896]{1,0:T(8,128)(2,1)} %collective-permute-done, pred[]{:T(512)S(6)} %eq.108), kind=kLoop, calls=%fused_computation.53 | loop fusion | flops 3670016 | bytes 14680065 | tf_op jit(solution)/shard_map/jit(_where)/select_n | solution.py:108
  265.7 11.9 %fusion.29 = bf16[1024,1792]{1,0:T(8,128)(2,1)S(1)} fusion(bf16[1024,2048]{0,1:T(8,128)(2,1)} %all-gather.6.cloned.1.call-done, bf16[2048,896]{1,0:T(8,128)(2,1)} %get-tuple-element.328, bf16[2048,896]{1,0:T(8,128)(2,1)} %get-tuple-element.327), kind=kOutput, calls=%fused_computation.46 | convolution fusion | flops 7532707840 | bytes 15204352 | tf_op jit(solution)/shard_map/dot_general | solution.py:112
  279.7 41.2 %reduce-scatter.3.cloned.1.call-done = bf16[256,1792]{1,0:T(8,128)(2,1)} async-done(((bf16[1024,1792]{1,0:T(8,128)(2,1)}), bf16[256,1792]{1,0:T(8,128)(2,1)}) %reduce-scatter.3.cloned.1.call-update) | async-done | bytes 917520 | tf_op jit(solution)/shard_map/reduce_scatter | solution.py:117
  320.9 4.6 all-to-all-start
  325.9 22.5 %all-to-all-done = bf16[4,64,1792]{2,1,0:T(8,128)(2,1)S(1)} async-done(((bf16[4,64,1792]{2,1,0:T(8,128)(2,1)}), bf16[4,64,1792]{2,1,0:T(8,128)(2,1)S(1)}, u32[]{:S(2)}, u32[]{:S(2)}) %all-to-all-start) | async-done | bytes 917536 | tf_op jit(solution)/shard_map/all_to_all | solution.py:123
  350.4 11.2 %all_to_all.15 = bf16[4,8,7168]{2,1,0:T(8,128)(2,1)} all-to-all(bf16[4,8,7168]{2,1,0:T(8,128)(2,1)S(1)} %convolution_convert_fusion.1), channel_id=1, replica_groups=mesh['ctx'=8,'exp'=4] {'exp'}, dimensions={0} | all-to-all | bytes 917504 | tf_op jit(solution)/shard_map/all_to_all | solution.py:151
  361.9 64.8 %all-gather.8.cloned.1.call-done = bf16[256,7168]{1,0:T(8,128)(2,1)} async-done(((bf16[32,7168]{1,0:T(8,128)(2,1)}), bf16[256,7168]{1,0:T(8,128)(2,1)}) %all-gather.8.cloned.1.call-update) | async-done | bytes 3670032 | tf_op jit(solution)/shard_map/all_gather | solution.py:153
  426.7 4.3 fusion.35
  431.0 10.0 %convolution_convert_fusion = bf16[256,7168]{1,0:T(8,128)(2,1)} fusion(bf16[1,256,7168]{2,1,0:T(8,128)(2,1)} %param.27, bf16[256,7168]{1,0:T(8,128)(2,1)} %all-gather.8.cloned.1.call-done, bf16[1,7168,256]{2,1,0:T(8,128)(2,1)} %param.26, f32[256,256]{1,0:T(8,128)S(1)} %fusion.35), kind=kOutput, calls=%fused_computation.37 | convolution fusion | flops 1881276416 | bytes 14942208 | tf_op jit(solution)/shard_map/dot_general | solution.py:158
  441.1 79.5 %reduce-scatter.5.cloned.1.call-done = bf16[32,7168]{1,0:T(8,128)(2,1)} async-done(((bf16[256,7168]{1,0:T(8,128)(2,1)}), bf16[32,7168]{1,0:T(8,128)(2,1)}) %reduce-scatter.5.cloned.1.call-update) | async-done | bytes 458768 | tf_op jit(solution)/shard_map/reduce_scatter | solution.py:157
  524.2 8.0 %all-to-all-done.2 = bf16[4,8,7168]{2,1,0:T(8,128)(2,1)S(1)} async-done(((bf16[4,8,7168]{2,1,0:T(8,128)(2,1)}), bf16[4,8,7168]{2,1,0:T(8,128)(2,1)S(1)}, u32[]{:S(2)}, u32[]{:S(2)}) %all-to-all-start.2) | async-done | bytes 458784 | tf_op jit(solution)/shard_map/all_to_all | solution.py:164
  (113 shorter events, 48.2 us)
Async XLA Ops:
  7.2 167.7 %copy-start = (bf16[16,512,128]{2,1,0:T(8,128)(2,1)S(1)}, bf16[16,512,128]{2,1,0:T(8,128)(2,1)}, u32[]{:S(2)}) copy-start(bf16[16,512,128]{2,1,0:T(8,128)(2,1)} %param.19) | copy-start | bytes 6291460
  7.2 61.0 %all-gather.4.cloned.1.call-start = ((), (), s32[]{:S(2)}) async-start(), calls=%async_computation.5 | async-start | bytes 2949120 | tf_op jit(solution)/shard_map/all_gather | solution.py:87
  9.2 256.5 %all-gather.6.cloned.1.call-start = ((), (), s32[]{:S(2)}) async-start(), calls=%async_computation.6 | async-start | bytes 5242880 | tf_op jit(solution)/shard_map/all_gather | solution.py:111
  9.3 9.0 %copy-start.6 = (s32[16]{0:T(128)S(1)}, s32[16]{0:T(128)}, u32[]{:S(2)}) copy-start(s32[16]{0:T(128)} %param.18) | copy-start | bytes 196
  77.2 7.3 %copy-start.1 = (pred[4096,512]{0,1:T(32,128)(4,1)S(1)}, pred[4096,512]{0,1:T(32,128)(4,1)}, u32[]{:S(2)}) copy-start(pred[4096,512]{0,1:T(32,128)(4,1)} %get-tuple-element.257) | copy-start | bytes 6291460 | tf_op jit(solution)/shard_map/while/body/eval_jaxpr/cond
  84.5 3.4 copy-start.2
  93.9 3.2 copy-start.3
  101.8 7.3 %copy-start.1 = (pred[4096,512]{0,1:T(32,128)(4,1)S(1)}, pred[4096,512]{0,1:T(32,128)(4,1)}, u32[]{:S(2)}) copy-start(pred[4096,512]{0,1:T(32,128)(4,1)} %get-tuple-element.257) | copy-start | bytes 6291460 | tf_op jit(solution)/shard_map/while/body/eval_jaxpr/cond
  109.1 3.4 copy-start.2
  118.4 3.2 copy-start.3
  126.3 7.3 %copy-start.1 = (pred[4096,512]{0,1:T(32,128)(4,1)S(1)}, pred[4096,512]{0,1:T(32,128)(4,1)}, u32[]{:S(2)}) copy-start(pred[4096,512]{0,1:T(32,128)(4,1)} %get-tuple-element.257) | copy-start | bytes 6291460 | tf_op jit(solution)/shard_map/while/body/eval_jaxpr/cond
  133.7 3.4 copy-start.2
  143.0 3.2 copy-start.3
  150.9 7.3 %copy-start.1 = (pred[4096,512]{0,1:T(32,128)(4,1)S(1)}, pred[4096,512]{0,1:T(32,128)(4,1)}, u32[]{:S(2)}) copy-start(pred[4096,512]{0,1:T(32,128)(4,1)} %get-tuple-element.257) | copy-start | bytes 6291460 | tf_op jit(solution)/shard_map/while/body/eval_jaxpr/cond
  158.2 3.4 copy-start.2
  167.6 3.2 copy-start.3
  178.6 142.3 %reduce-scatter.3.cloned.1.call-start = ((), (), s32[]{:S(2)}) async-start(), calls=%async_computation.7 | async-start | bytes 4587520 | tf_op jit(solution)/shard_map/reduce_scatter | solution.py:117
  178.6 80.2 %collective-permute-start = (bf16[2048,896]{1,0:T(8,128)(2,1)}, bf16[2048,896]{1,0:T(8,128)(2,1)}, u32[]{:S(2)}, u32[]{:S(2)}) collective-permute-start(bf16[2048,896]{1,0:T(8,128)(2,1)} %param.20), channel_id=1, source_target_pairs={{0,4},{4,0},{8,12},{12,8},{16,20},{20,16},{24,28},{28,24},{1,5},{5... | collective-permute-start | bytes 11010056 | tf_op jit(solution)/shard_map/ppermute | solution.py:105
  279.6 45.9 %copy-start.9 = (bf16[7168]{0:T(1024)(128)(2,1)S(1)}, bf16[7168]{0:T(1024)(128)(2,1)}, u32[]{:S(2)}) copy-start(bf16[7168]{0:T(1024)(128)(2,1)} %param.22) | copy-start | bytes 43012
  279.6 45.9 %copy-start.8 = (s32[64,8]{0,1:T(8,128)S(1)}, s32[64,8]{0,1:T(8,128)}, u32[]{:S(2)}) copy-start(s32[64,8]{0,1:T(8,128)} %param.23) | copy-start | bytes 6148
  320.9 27.5 %all-to-all-start = ((bf16[4,64,1792]{2,1,0:T(8,128)(2,1)}), bf16[4,64,1792]{2,1,0:T(8,128)(2,1)S(1)}, u32[]{:S(2)}, u32[]{:S(2)}) async-start(bf16[4,64,1792]{2,1,0:T(8,128)(2,1)} %bitcast.57), calls=%async_computation.1 | async-start | bytes 1835008 | tf_op jit(solution)/shard_map/all_to_all | solution.py:123
  325.5 101.3 %all-gather.8.cloned.1.call-start = ((), (), s32[]{:S(2)}) async-start(), calls=%async_computation.8 | async-start | bytes 4128768 | tf_op jit(solution)/shard_map/all_gather | solution.py:153
  348.4 1.2 copy-start.4
  349.9 81.1 %copy-start.5 = (bf16[64,7168]{1,0:T(8,128)(2,1)}, bf16[64,7168]{1,0:T(8,128)(2,1)S(1)}, u32[]{:S(2)}) copy-start(bf16[64,7168]{1,0:T(8,128)(2,1)S(1)} %get-tuple-element.322) | copy-start | bytes 2752516
  361.6 158.9 %reduce-scatter.5.cloned.1.call-start = ((), (), s32[]{:S(2)}) async-start(), calls=%async_computation.9 | async-start | bytes 4128768 | tf_op jit(solution)/shard_map/reduce_scatter | solution.py:157
  441.1 83.0 %copy-start.7 = (f32[64,8]{0,1:T(8,128)S(1)}, f32[64,8]{0,1:T(8,128)}, u32[]{:S(2)}) copy-start(f32[64,8]{0,1:T(8,128)} %param.24) | copy-start | bytes 6148
  520.6 11.6 %all-to-all-start.2 = ((bf16[4,8,7168]{2,1,0:T(8,128)(2,1)}), bf16[4,8,7168]{2,1,0:T(8,128)(2,1)S(1)}, u32[]{:S(2)}, u32[]{:S(2)}) async-start(bf16[4,8,7168]{2,1,0:T(8,128)(2,1)} %bitcast.58), calls=%async_computation.4 | async-start | bytes 917504 | tf_op jit(solution)/shard_map/all_to_all | solution.py:164
Sparse Core Ops, SparseCore 0:
  10.8 57.3 all-gather.3
  178.7 79.1 all-gather.5
  279.8 41.0 reduce-scatter.2
  361.8 64.9 all-gather.7
  441.2 79.2 reduce-scatter.4

commit v2 on v1

--- a/solution.py
+++ b/solution.py
@@ -1,8 +1,10 @@
-import math
+import functools
 
 import jax
 import jax.numpy as jnp
 from jax import lax
+from jax.experimental import pallas as pl
+from jax.experimental.pallas import tpu as pltpu
 from jax.sharding import PartitionSpec as P
 
 EXPERTS = 256
@@ -18,38 +20,54 @@
     return first * BLK + rows % BLK
 
 
-def attend(carry, piece, flat_query, query_place, block_order, scale, latent_width):
-    length = piece.shape[0]
-    part = math.gcd(length, 512)
+def attend_heads(scale, query_ref, keys_ref, flipped_ref, query_place_ref, key_place_ref, w_uv_ref, out_ref):
+    width = flipped_ref.shape[0]
+    latent_width, value_width = w_uv_ref.shape[1:]
+    allowed = key_place_ref[...] <= query_place_ref[...]
+    for head in range(w_uv_ref.shape[0]):
+        query = query_ref[:, head * width : (head + 1) * width]
+        scores = jnp.dot(query, flipped_ref[...], preferred_element_type=jnp.float32) * scale
+        scores = jnp.where(allowed, scores, -1e30)
+        highest = jnp.max(scores, axis=1, keepdims=True)
+        weights = jnp.exp(scores - highest)
+        total = jnp.sum(weights, axis=1, keepdims=True)
+        mixed = jnp.dot(
+            weights.astype(jnp.bfloat16),
+            keys_ref[:, :latent_width],
+            preferred_element_type=jnp.float32,
+        )
+        attn_latent = (mixed / total).astype(jnp.bfloat16)
+        out_ref[:, head * value_width : (head + 1) * value_width] = jnp.dot(
+            attn_latent, w_uv_ref[head], preferred_element_type=jnp.float32
+        ).astype(jnp.bfloat16)
 
-    def one_part(index, state):
-        keys = lax.dynamic_slice_in_dim(piece, index * part, part, 0)
-        offset = index * part + jnp.arange(part, dtype=jnp.int32)
-        allowed = block_places(block_order, offset)[None, :] <= query_place[:, None]
 
-        def update(inner):
-            highest, total, weighted = inner
-            scores = (
-                lax.dot_general(
-                    flat_query, keys, (((1,), (1,)), ((), ())), preferred_element_type=jnp.float32
-                )
-                * scale
-            )
-            scores = jnp.where(allowed, scores, -1e30)
-            newest = jnp.maximum(highest, jnp.max(scores, axis=1))
-            shrink = jnp.exp(highest - newest)
-            weights = jnp.where(allowed, jnp.exp(scores - newest[:, None]), 0.0)
-            total = total * shrink + jnp.sum(weights, axis=1)
-            weighted = weighted * shrink[:, None] + jnp.dot(
-                weights.astype(jnp.bfloat16),
-                keys[:, :latent_width],
-                preferred_element_type=jnp.float32,
-            )
-            return (newest, total, weighted)
-
-        return lax.cond(jnp.any(allowed), update, lambda inner: inner, state)
-
-    return lax.fori_loop(0, length // part, one_part, carry)
+def attention(queries, keys, query_place, key_place, w_uv, scale):
+    rows = queries.shape[0]
+    head_count, latent_width, value_width = w_uv.shape
+    length, width = keys.shape
+    group = 2
+    whole = lambda step: (0, 0)
+    return pl.pallas_call(
+        functools.partial(attend_heads, scale),
+        grid=(head_count // group,),
+        out_shape=jax.ShapeDtypeStruct((rows, head_count * value_width), jnp.bfloat16),
+        in_specs=[
+            pl.BlockSpec((rows, group * width), lambda step: (0, step)),
+            pl.BlockSpec((length, width), whole),
+            pl.BlockSpec((width, length), whole),
+            pl.BlockSpec((rows, 1), whole),
+            pl.BlockSpec((1, length), whole),
+            pl.BlockSpec((group, latent_width, value_width), lambda step: (step, 0, 0)),
+        ],
+        out_specs=pl.BlockSpec((rows, group * value_width), lambda step: (0, step)),
+        compiler_params=pltpu.CompilerParams(vmem_limit_bytes=52 * 2**20),
+        cost_estimate=pl.CostEstimate(
+            flops=2 * rows * length * head_count * (width + latent_width),
+            bytes_accessed=2 * rows * head_count * (width + value_width),
+            transcendentals=rows * length * head_count,
+        ),
+    )(queries, keys, keys.T, query_place[:, None], key_place[None, :], w_uv)
 
 
 def per_device(
@@ -74,39 +92,14 @@
     model_width = residual.shape[1]
     scale = (value_width + key_width - latent_width) ** (-0.5)
     rows_here = lax.axis_index("ctx") * seq_block + jnp.arange(seq_block, dtype=jnp.int32)
-    query_place = jnp.repeat(block_places(block_order, rows_here), head_count)
-    flat_query = queries.reshape(seq_block * head_count, key_width)
-    query_rows = seq_block * head_count
-    start_state = (
-        jnp.full((query_rows,), -1e30, jnp.float32),
-        jnp.zeros((query_rows,), jnp.float32),
-        jnp.zeros((query_rows, latent_width), jnp.float32),
-    )
-    highest, total, weighted = attend(
-        start_state,
-        lax.all_gather(latent, "ctx", axis=0, tiled=True),
-        flat_query,
-        query_place,
-        block_order,
-        scale,
-        latent_width,
-    )
-    attn_latent = (
-        (weighted / total[:, None])
-        .astype(jnp.bfloat16)
-        .reshape(seq_block, head_count, latent_width)
-    )
-    heads = jnp.einsum(
-        "thl,hlv->thv", attn_latent, w_uv, preferred_element_type=jnp.float32
-    ).astype(jnp.bfloat16)
-    heads = heads.reshape(seq_block, head_count * value_width)
+    query_place = block_places(block_order, rows_here)
+    keys = lax.all_gather(latent, "ctx", axis=0, tiled=True)
+    key_place = block_places(block_order, jnp.arange(keys.shape[0], dtype=jnp.int32))
+    heads = attention(queries, keys, query_place, key_place, w_uv, scale)
     ctx_count = lax.axis_size("ctx")
     levels = ctx_count // PAIR
-    other = lax.ppermute(w_o, "ctx", [(c, c ^ 1) for c in range(ctx_count)])
-    first = lax.axis_index("ctx") % PAIR == 0
-    pair_columns = jnp.concatenate(
-        [jnp.where(first, w_o, other), jnp.where(first, other, w_o)], axis=1
-    )
+    pairs = [[level * PAIR + side for side in range(PAIR)] for level in range(levels)]
+    pair_columns = lax.all_gather(w_o, "ctx", axis=1, tiled=True, axis_index_groups=pairs)
     lines = [[level * PAIR + side for level in range(levels)] for side in range(PAIR)]
     line_heads = lax.all_gather(heads, "ctx", axis=0, tiled=True, axis_index_groups=lines)
     terms = jnp.dot(line_heads, pair_columns, preferred_element_type=jnp.float32).astype(

time: 542 us -> 514 us (0.948)
  waiting for transfers between devices: 345 us -> 406 us
  matrix products: 85.4 us -> 28.5 us
  Pallas kernels: 0 us -> 37.3 us
  other arithmetic: 37.4 us -> 1.16 us
  local copies, waits for them, and re-layouts: 35.3 us -> 6.87 us
    all_gather x1, waiting for transfers between devices: 0.01 us -> 82.4 us  [per_device(): lax.all_gather(heads, 'ctx', axis=0, tiled=True, axis_index_groups=lines)]
    ppermute x1 -> x0, waiting for transfers between devices: 79.6 us -> none  [per_device(): other = lax.ppermute(w_o, 'ctx', [(c, c ^ 1) for c in range(ctx_count)])]
    all_gather x1 -> x2, waiting for transfers between devices: 49.8 us -> 108 us  [the longest x1 57.3 us: per_device(): keys = lax.all_gather(latent, 'ctx', axis=0, tiled=True)]
    dot_general x9 -> x0, matrix products: 56.6 us -> none  [the longest x4 29.1 us: update(): lax.dot_general(flat_query, keys, (((1,), (1,)), ((), ())), preferred_ele...]
    pallas_call x0 -> x1, Pallas kernels: none -> 37.3 us  [attention(): pl.pallas_call(functools.partial(attend_heads, scale), grid=(head_count /...]
    cond x28 -> x0, local copies, waits for them, and re-layouts: 16 us -> none
    le x4 -> x0, other arithmetic: 14.8 us -> none  [one_part(): allowed = block_places(block_order, offset)[None, :] <= query_place[:, None]]
    reduce_sum x4 -> x0, other arithmetic: 10.2 us -> none  [update(): total = total * shrink + jnp.sum(weights, axis=1)]
  transfers between devices with their start and end apart: 8 -> 8, of which waited for: 7 -> 8; matrix products, arithmetic and copies ran while one was open for 3% -> 1% of each run, Pallas kernels for 0% -> 7%
where the time goes in v2:
time: 514 us
  waiting for transfers between devices  406 us (79%)
  Pallas kernels  37.3 us (7%)
  matrix products  28.5 us (6%)
  between operations  14.3 us (3%)
  blocking collectives  11.2 us (2%)
  starting transfers between devices  8.45 us (2%)
  local copies, waits for them, and re-layouts  6.87 us (1%)
    all_gather x1, waiting for transfers between devices, per_device(): lax.all_gather(heads, 'ctx', axis=0, tiled=True, axis_index_groups=lines)  82.4 us
    reduce_scatter x1, waiting for transfers between devices, per_device(): lax.psum_scatter(jnp.dot(hidden, w_down[0], preferred_element_type=jnp.fl...  79.3 us
    all_gather x1, waiting for transfers between devices, per_device(): piece = lax.all_gather(flat_rows, 'ctx', axis=0, tiled=True)  64.9 us
    all_gather x1, waiting for transfers between devices, per_device(): keys = lax.all_gather(latent, 'ctx', axis=0, tiled=True)  57.3 us
    all_gather x1, waiting for transfers between devices, per_device(): lax.all_gather(w_o, 'ctx', axis=1, tiled=True, axis_index_groups=pairs)  50.3 us
    reduce_scatter x1, waiting for transfers between devices, per_device(): lax.psum_scatter(terms.reshape(owner_count * levels * token_count, width)...  39.9 us
    pallas_call x1, Pallas kernels, attention(): pl.pallas_call(functools.partial(attend_heads, scale), grid=(head_count /...  37.3 us
    all_to_all x1, waiting for transfers between devices, per_device(): lax.all_to_all(summed, 'ctx', split_axis=0, concat_axis=0, tiled=True, ax...  22.5 us
  transfers between devices with their start and end apart: 8, of which 8 were waited for; matrix products, arithmetic and copies ran while one was open for 1% of the time, Pallas kernels for 7%

profile of v2, /device:TPU:0, one launch (start us, length us, event | category | flops | bytes accessed | tf_op | source)
XLA Modules:
  0.0 513.9 jit_solution(5995561231421837497)
XLA Ops:
  7.2 0.7 all-gather.5.cloned.1.call-update
  8.0 0.7 all-gather.9.cloned.1.call-update
  8.7 0.1 select_reduce_fusion.1
  8.8 0.1 copy.34
  9.0 0.1 select_reduce_fusion
  9.2 57.3 %all-gather.5.cloned.1.call-done = bf16[2048,576]{0,1:T(8,128)(2,1)} async-done(((bf16[256,576]{0,1:T(8,128)(2,1)}), bf16[2048,576]{0,1:T(8,128)(2,1)}) %all-gather.5.cloned.1.call-update) | async-done | bytes 2359312 | tf_op jit(solution)/shard_map/all_gather | solution.py:96
  66.5 4.3 copy.35.keys_ref
  70.8 37.3 %shard_map.131 = bf16[256,2048]{1,0:T(8,128)(2,1)} custom-call(bf16[256,9216]{1,0:T(8,128)(2,1)} %query_ref.1, bf16[2048,576]{1,0:T(8,128)(2,1)} %copy.35.keys_ref, bf16[576,2048]{1,0:T(8,128)(2,1)} %bitcast.41, s32[256,1]{1,0:T(8,128)S(1)} %fusion.27.query_place_ref, s32[1,2048]{1,0:T(1,128)S(1)} %fusion.37.key_place_ref, bf16[16,512,128]{2,1,0:T(8,128)(2,1)} %w_uv_ref.1), custom_call_target="tpu_custom_call" | custom-call | flops 18253611008 | bytes 5767168 | tf_op jit(solution)/shard_map/pallas_call | solution.py:51
  108.2 50.3 %all-gather.9.cloned.1.call-done = bf16[2048,1792]{1,0:T(8,128)(2,1)} async-done(((bf16[2048,896]{1,0:T(8,128)(2,1)}), bf16[2048,1792]{1,0:T(8,128)(2,1)}) %all-gather.9.cloned.1.call-update) | async-done | bytes 7340048 | tf_op jit(solution)/shard_map/all_gather | solution.py:102
  158.5 82.4 %all-gather.7.cloned.1.call-done = bf16[1024,2048]{1,0:T(8,128)(2,1)} async-done(((bf16[256,2048]{1,0:T(8,128)(2,1)}), bf16[1024,2048]{1,0:T(8,128)(2,1)}) %all-gather.7.cloned.1.call-update) | async-done | bytes 4194320 | tf_op jit(solution)/shard_map/all_gather | solution.py:104
  240.9 11.7 %convolution_convert_fusion.2 = bf16[1024,1792]{1,0:T(8,128)(2,1)S(1)} fusion(bf16[1024,2048]{1,0:T(8,128)(2,1)} %all-gather.7.cloned.1.call-done, bf16[2048,1792]{1,0:T(8,128)(2,1)} %all-gather.9.cloned.1.call-done), kind=kOutput, calls=%fused_computation.3 | convolution fusion | flops 7518027776 | bytes 15204352 | tf_op jit(solution)/shard_map/dot_general | solution.py:105
  252.5 2.1 copy.36
  254.6 39.9 %reduce-scatter.3.cloned.1.call-done = bf16[256,1792]{1,0:T(8,128)(2,1)} async-done(((bf16[1024,1792]{1,0:T(8,128)(2,1)}), bf16[256,1792]{1,0:T(8,128)(2,1)}) %reduce-scatter.3.cloned.1.call-update) | async-done | bytes 917520 | tf_op jit(solution)/shard_map/reduce_scatter | solution.py:110
  294.6 4.6 all-to-all-start
  299.2 0.1 fusion.32
  299.3 0.1 copy.38
  299.4 0.1 reduce_window_sum.11
  299.6 22.5 %all-to-all-done = bf16[4,64,1792]{2,1,0:T(8,128)(2,1)S(1)} async-done(((bf16[4,64,1792]{2,1,0:T(8,128)(2,1)}), bf16[4,64,1792]{2,1,0:T(8,128)(2,1)S(1)}, u32[]{:S(2)}, u32[]{:S(2)}) %all-to-all-start) | async-done | bytes 917536 | tf_op jit(solution)/shard_map/all_to_all | solution.py:116
  322.1 0.1 convert_bitcast_fusion
  322.2 0.1 copy.40
  322.4 0.4 fusion.6
  322.8 0.4 convolution_convert_fusion.1
  323.2 11.2 %all_to_all.15 = bf16[4,8,7168]{2,1,0:T(8,128)(2,1)} all-to-all(bf16[4,8,7168]{2,1,0:T(8,128)(2,1)S(1)} %convolution_convert_fusion.1), channel_id=1, replica_groups=mesh['ctx'=8,'exp'=4] {'exp'}, dimensions={0} | all-to-all | bytes 917504 | tf_op jit(solution)/shard_map/all_to_all | solution.py:144
  334.5 0.2 reduce-scatter.5.cloned.1.call-start
  334.7 64.9 %all-gather.11.cloned.1.call-done = bf16[256,7168]{1,0:T(8,128)(2,1)} async-done(((bf16[32,7168]{1,0:T(8,128)(2,1)}), bf16[256,7168]{1,0:T(8,128)(2,1)}) %all-gather.11.cloned.1.call-update) | async-done | bytes 3670032 | tf_op jit(solution)/shard_map/all_gather | solution.py:146
  399.6 4.3 fusion.3
  403.9 10.0 %convolution_convert_fusion = bf16[256,7168]{1,0:T(8,128)(2,1)} fusion(bf16[1,256,7168]{2,1,0:T(8,128)(2,1)} %param.23, bf16[256,7168]{1,0:T(8,128)(2,1)} %all-gather.11.cloned.1.call-done, bf16[1,7168,256]{2,1,0:T(8,128)(2,1)} %param.22, f32[256,256]{1,0:T(8,128)S(1)} %fusion.3), kind=kOutput, calls=%fused_computation.1 | convolution fusion | flops 1881276416 | bytes 14942208 | tf_op jit(solution)/shard_map/dot_general | solution.py:151
  413.9 79.3 %reduce-scatter.5.cloned.1.call-done = bf16[32,7168]{1,0:T(8,128)(2,1)} async-done(((bf16[256,7168]{1,0:T(8,128)(2,1)}), bf16[32,7168]{1,0:T(8,128)(2,1)}) %reduce-scatter.5.cloned.1.call-update) | async-done | bytes 458768 | tf_op jit(solution)/shard_map/reduce_scatter | solution.py:150
  493.3 3.5 all-to-all-start.2
  496.8 0.1 fusion.33
  496.9 8.0 %all-to-all-done.2 = bf16[4,8,7168]{2,1,0:T(8,128)(2,1)S(1)} async-done(((bf16[4,8,7168]{2,1,0:T(8,128)(2,1)}), bf16[4,8,7168]{2,1,0:T(8,128)(2,1)S(1)}, u32[]{:S(2)}, u32[]{:S(2)}) %all-to-all-start.2) | async-done | bytes 458784 | tf_op jit(solution)/shard_map/all_to_all | solution.py:157
  504.9 2.1 fusion.5
  (35 shorter events, 0.5 us)
Async XLA Ops:
  7.2 1.6 copy-start.5
  7.2 59.4 %all-gather.5.cloned.1.call-start = ((), (), s32[]{:S(2)}) async-start(), calls=%async_computation.5 | async-start | bytes 2654208 | tf_op jit(solution)/shard_map/all_gather | solution.py:96
  7.9 150.6 %all-gather.9.cloned.1.call-start = ((), (), s32[]{:S(2)}) async-start(), calls=%async_computation.7 | async-start | bytes 11010048 | tf_op jit(solution)/shard_map/all_gather | solution.py:102
  8.7 232.2 %all-gather.7.cloned.1.call-start = ((), (), s32[]{:S(2)}) async-start(), calls=%async_computation.6 | async-start | bytes 5242880 | tf_op jit(solution)/shard_map/all_gather | solution.py:104
  108.2 186.4 %reduce-scatter.3.cloned.1.call-start = ((), (), s32[]{:S(2)}) async-start(), calls=%async_computation.8 | async-start | bytes 4587520 | tf_op jit(solution)/shard_map/reduce_scatter | solution.py:110
  254.6 44.6 %copy-start.3 = (s32[64,8]{0,1:T(8,128)S(1)}, s32[64,8]{0,1:T(8,128)}, u32[]{:S(2)}) copy-start(s32[64,8]{0,1:T(8,128)} %param.19) | copy-start | bytes 6148
  254.6 44.9 %copy-start.4 = (bf16[7168]{0:T(1024)(128)(2,1)S(1)}, bf16[7168]{0:T(1024)(128)(2,1)}, u32[]{:S(2)}) copy-start(bf16[7168]{0:T(1024)(128)(2,1)} %param.18) | copy-start | bytes 43012
  294.6 27.5 %all-to-all-start = ((bf16[4,64,1792]{2,1,0:T(8,128)(2,1)}), bf16[4,64,1792]{2,1,0:T(8,128)(2,1)S(1)}, u32[]{:S(2)}, u32[]{:S(2)}) async-start(bf16[4,64,1792]{2,1,0:T(8,128)(2,1)} %bitcast.43), calls=%async_computation.1 | async-start | bytes 1835008 | tf_op jit(solution)/shard_map/all_to_all | solution.py:116
  299.2 23.2 %copy-start = (bf16[64,7168]{1,0:T(8,128)(2,1)S(1)}, bf16[64,7168]{1,0:T(8,128)(2,1)}, u32[]{:S(2)}) copy-start(bf16[64,7168]{1,0:T(8,128)(2,1)} %param.17) | copy-start | bytes 2752516
  299.2 100.4 %all-gather.11.cloned.1.call-start = ((), (), s32[]{:S(2)}) async-start(), calls=%async_computation.9 | async-start | bytes 4128768 | tf_op jit(solution)/shard_map/all_gather | solution.py:146
  322.8 81.1 %copy-start.1 = (bf16[64,7168]{1,0:T(8,128)(2,1)}, bf16[64,7168]{1,0:T(8,128)(2,1)S(1)}, u32[]{:S(2)}) copy-start(bf16[64,7168]{1,0:T(8,128)(2,1)S(1)} %get-tuple-element.3) | copy-start | bytes 2752516
  334.5 158.8 %reduce-scatter.5.cloned.1.call-start = ((), (), s32[]{:S(2)}) async-start(), calls=%async_computation.10 | async-start | bytes 4128768 | tf_op jit(solution)/shard_map/reduce_scatter | solution.py:150
  413.9 82.8 %copy-start.2 = (f32[64,8]{0,1:T(8,128)S(1)}, f32[64,8]{0,1:T(8,128)}, u32[]{:S(2)}) copy-start(f32[64,8]{0,1:T(8,128)} %param.20) | copy-start | bytes 6148
  493.3 11.6 %all-to-all-start.2 = ((bf16[4,8,7168]{2,1,0:T(8,128)(2,1)}), bf16[4,8,7168]{2,1,0:T(8,128)(2,1)S(1)}, u32[]{:S(2)}, u32[]{:S(2)}) async-start(bf16[4,8,7168]{2,1,0:T(8,128)(2,1)} %bitcast.44), calls=%async_computation.4 | async-start | bytes 917504 | tf_op jit(solution)/shard_map/all_to_all | solution.py:157
Sparse Core Ops, SparseCore 0:
  10.1 56.4 all-gather.4
  68.1 90.3 all-gather.8
  160.1 80.7 all-gather.6
  254.8 39.7 reduce-scatter.2
  334.6 64.9 all-gather.10
  414.1 79.1 reduce-scatter.4

commit v3 on v2

--- a/solution.py
+++ b/solution.py
@@ -11,6 +11,7 @@
 TOP = 8
 BLK = 128
 PAIR = 2
+HALVES = 2
 
 
 def block_places(block_order, rows):
@@ -42,23 +43,25 @@
         ).astype(jnp.bfloat16)
 
 
-def attention(queries, keys, query_place, key_place, w_uv, scale):
+def attention(queries, keys, query_place, key_place, w_uv, scale, part, parts):
     rows = queries.shape[0]
     head_count, latent_width, value_width = w_uv.shape
     length, width = keys.shape
     group = 2
+    head_count = head_count // parts
+    first = part * (head_count // group)
     whole = lambda step: (0, 0)
     return pl.pallas_call(
         functools.partial(attend_heads, scale),
         grid=(head_count // group,),
         out_shape=jax.ShapeDtypeStruct((rows, head_count * value_width), jnp.bfloat16),
         in_specs=[
-            pl.BlockSpec((rows, group * width), lambda step: (0, step)),
+            pl.BlockSpec((rows, group * width), lambda step: (0, first + step)),
             pl.BlockSpec((length, width), whole),
             pl.BlockSpec((width, length), whole),
             pl.BlockSpec((rows, 1), whole),
             pl.BlockSpec((1, length), whole),
-            pl.BlockSpec((group, latent_width, value_width), lambda step: (step, 0, 0)),
+            pl.BlockSpec((group, latent_width, value_width), lambda step: (first + step, 0, 0)),
         ],
         out_specs=pl.BlockSpec((rows, group * value_width), lambda step: (0, step)),
         compiler_params=pltpu.CompilerParams(vmem_limit_bytes=52 * 2**20),
@@ -95,16 +98,19 @@
     query_place = block_places(block_order, rows_here)
     keys = lax.all_gather(latent, "ctx", axis=0, tiled=True)
     key_place = block_places(block_order, jnp.arange(keys.shape[0], dtype=jnp.int32))
-    heads = attention(queries, keys, query_place, key_place, w_uv, scale)
     ctx_count = lax.axis_size("ctx")
     levels = ctx_count // PAIR
-    pairs = [[level * PAIR + side for side in range(PAIR)] for level in range(levels)]
-    pair_columns = lax.all_gather(w_o, "ctx", axis=1, tiled=True, axis_index_groups=pairs)
     lines = [[level * PAIR + side for level in range(levels)] for side in range(PAIR)]
-    line_heads = lax.all_gather(heads, "ctx", axis=0, tiled=True, axis_index_groups=lines)
-    terms = jnp.dot(line_heads, pair_columns, preferred_element_type=jnp.float32).astype(
-        jnp.bfloat16
-    )
+    other = lax.ppermute(w_o, "ctx", [(c, c ^ 1) for c in range(ctx_count)])
+    depth = w_o.shape[0] // HALVES
+    own_terms, other_terms = 0.0, 0.0
+    for part in range(HALVES):
+        heads = attention(queries, keys, query_place, key_place, w_uv, scale, part, HALVES)
+        heads = lax.all_gather(heads, "ctx", axis=0, tiled=True, axis_index_groups=lines)
+        rows = slice(part * depth, (part + 1) * depth)
+        own_terms += jnp.dot(heads, w_o[rows], preferred_element_type=jnp.float32)
+        other_terms += jnp.dot(heads, other[rows], preferred_element_type=jnp.float32)
+    terms = jnp.concatenate([own_terms, other_terms], axis=1).astype(jnp.bfloat16)
     width = terms.shape[1]
     terms = jnp.swapaxes(terms.reshape(levels, owner_count, token_count, width), 0, 1)
     summed = lax.psum_scatter(
@@ -116,9 +122,9 @@
     spread = lax.all_to_all(
         summed, "ctx", split_axis=0, concat_axis=0, tiled=True, axis_index_groups=lines
     )
-    projected = (
-        jnp.swapaxes(spread, 0, 1).reshape(token_count, model_width).astype(jnp.float32)
-    )
+    spread = jnp.swapaxes(spread, 0, 1).reshape(token_count, levels, PAIR, width // PAIR)
+    spread = jnp.where(lax.axis_index("ctx") % PAIR == 0, spread, spread[:, :, ::-1])
+    projected = spread.reshape(token_count, model_width).astype(jnp.float32)
     attended = (residual.astype(jnp.float32) + projected).astype(jnp.bfloat16)
     level = attended.astype(jnp.float32)
     normed = (

time: 514 us -> 460 us (0.89)
  waiting for transfers between devices: 406 us -> 330 us
  matrix products: 28.5 us -> 38.6 us
    all_gather x1 -> x2, waiting for transfers between devices: 82.4 us -> 26.5 us  [per_device(): lax.all_gather(heads, 'ctx', axis=0, tiled=True, axis_index_groups=lines)]
    all_gather x1 -> x0, waiting for transfers between devices: 50.3 us -> none  [per_device(): lax.all_gather(w_o, 'ctx', axis=1, tiled=True, axis_index_groups=pairs)]
    ppermute x0 -> x1, waiting for transfers between devices: none -> 30.6 us  [per_device(): other = lax.ppermute(w_o, 'ctx', [(c, c ^ 1) for c in range(ctx_count)])]
    dot_general x1 -> x4, matrix products: 11.7 us -> 21.7 us  [the longest x2 12.2 us: per_device(): own_terms += jnp.dot(heads, w_o[rows], preferred_element_type=jnp.float32)]
    pallas_call x1 -> x2, Pallas kernels: 37.3 us -> 39.9 us  [attention(): pl.pallas_call(functools.partial(attend_heads, scale), grid=(head_count /...]
  transfers between devices with their start and end apart: 8 -> 9, of which waited for: 8 -> 9; matrix products, arithmetic and copies ran while one was open for 1% -> 3% of each run, Pallas kernels for 7% -> 4%
where the time goes in v3:
time: 460 us; the launch traced here: 459 us
  waiting for transfers between devices  330 us (72%)
  Pallas kernels  39.9 us (9%)
  matrix products  38.6 us (8%)
  between operations  14.3 us (3%)
  blocking collectives  11.2 us (2%)
  local copies, waits for them, and re-layouts  11 us (2%)
  starting transfers between devices  10.2 us (2%)
    reduce_scatter x1, waiting for transfers between devices, per_device(): lax.psum_scatter(jnp.dot(hidden, w_down[0], preferred_element_type=jnp.fl...  79.5 us
    all_gather x1, waiting for transfers between devices, per_device(): piece = lax.all_gather(flat_rows, 'ctx', axis=0, tiled=True)  64.8 us
    all_gather x1, waiting for transfers between devices, per_device(): keys = lax.all_gather(latent, 'ctx', axis=0, tiled=True)  56.8 us
    reduce_scatter x1, waiting for transfers between devices, per_device(): lax.psum_scatter(terms.reshape(owner_count * levels * token_count, width)...  40.1 us
    pallas_call x2, Pallas kernels, attention(): pl.pallas_call(functools.partial(attend_heads, scale), grid=(head_count /...  39.9 us
    ppermute x1, waiting for transfers between devices, per_device(): other = lax.ppermute(w_o, 'ctx', [(c, c ^ 1) for c in range(ctx_count)])  30.6 us
    all_gather x2, waiting for transfers between devices, per_device(): lax.all_gather(heads, 'ctx', axis=0, tiled=True, axis_index_groups=lines)  26.5 us
    all_to_all x1, waiting for transfers between devices, per_device(): lax.all_to_all(summed, 'ctx', split_axis=0, concat_axis=0, tiled=True, ax...  22.5 us
  transfers between devices with their start and end apart: 9, of which 9 were waited for; matrix products, arithmetic and copies ran while one was open for 3% of the time, Pallas kernels for 4%

profile of v3, /device:TPU:0, one launch (start us, length us, event | category | flops | bytes accessed | tf_op | source)
XLA Modules:
  0.0 459.1 jit_solution(504049631891666259)
XLA Ops:
  7.2 0.7 all-gather.5.cloned.1.call-update
  8.0 0.7 select_reduce_fusion.1
  8.9 0.8 select_reduce_fusion
  9.7 56.8 %all-gather.5.cloned.1.call-done = bf16[2048,576]{0,1:T(8,128)(2,1)} async-done(((bf16[256,576]{0,1:T(8,128)(2,1)}), bf16[2048,576]{0,1:T(8,128)(2,1)}) %all-gather.5.cloned.1.call-update) | async-done | bytes 2359312 | tf_op jit(solution)/shard_map/all_gather | solution.py:99
  66.5 4.3 copy.46.keys_ref
  70.9 19.9 %shard_map.132 = bf16[256,1024]{1,0:T(8,128)(2,1)} custom-call(bf16[256,9216]{1,0:T(8,128)(2,1)} %query_ref.3, bf16[2048,576]{1,0:T(8,128)(2,1)} %copy.46.keys_ref, bf16[576,2048]{1,0:T(8,128)(2,1)} %bitcast.45, s32[256,1]{1,0:T(8,128)S(1)} %fusion.40.query_place_ref, s32[1,2048]{1,0:T(1,128)S(1)} %fusion.50.key_place_ref, bf16[16,512,128]{2,1,0:T(8,128)(2,1)} %w_uv_ref.3), custom_call_target="tpu_custom_call" | custom-call | flops 9126805504 | bytes 2883584 | tf_op jit(solution)/shard_map/pallas_call | solution.py:54
  90.9 1.5 collective-permute-start
  92.4 19.9 %shard_map.131 = bf16[256,1024]{1,0:T(8,128)(2,1)} custom-call(bf16[256,9216]{1,0:T(8,128)(2,1)} %query_ref.3, bf16[2048,576]{1,0:T(8,128)(2,1)} %copy.46.keys_ref, bf16[576,2048]{1,0:T(8,128)(2,1)} %bitcast.46, s32[256,1]{1,0:T(8,128)S(1)} %fusion.40.query_place_ref, s32[1,2048]{1,0:T(1,128)S(1)} %fusion.50.key_place_ref, bf16[16,512,128]{2,1,0:T(8,128)(2,1)} %w_uv_ref.3), custom_call_target="tpu_custom_call" | custom-call | flops 9126805504 | bytes 2883584 | tf_op jit(solution)/shard_map/pallas_call | solution.py:54
  112.6 22.5 %all-gather.9.cloned.1.call-done = bf16[1024,1024]{1,0:T(8,128)(2,1)} async-done(((bf16[256,1024]{1,0:T(8,128)(2,1)}), bf16[1024,1024]{1,0:T(8,128)(2,1)}) %all-gather.9.cloned.1.call-update) | async-done | bytes 2097168 | tf_op jit(solution)/shard_map/all_gather | solution.py:109
  135.1 6.5 %fusion.13 = f32[1024,896]{1,0:T(8,128)} fusion(bf16[1024,1024]{1,0:T(8,128)(2,1)} %all-gather.9.cloned.1.call-done, bf16[2048,896]{1,0:T(8,128)(2,1)} %param.16), kind=kOutput, calls=%fused_computation.22 | convolution fusion | flops 1879048192 | bytes 7602176 | tf_op jit(solution)/shard_map/dot_general | solution.py:111
  141.6 30.6 %collective-permute-done = bf16[2048,896]{1,0:T(8,128)(2,1)} collective-permute-done((bf16[2048,896]{1,0:T(8,128)(2,1)}, bf16[2048,896]{1,0:T(8,128)(2,1)}, u32[]{:S(2)}, u32[]{:S(2)}) %collective-permute-start) | collective-permute-done | bytes 3670048 | tf_op jit(solution)/shard_map/ppermute | solution.py:104
  172.2 5.7 %fusion.9 = f32[1024,896]{1,0:T(8,128)} fusion(bf16[1024,1024]{1,0:T(8,128)(2,1)S(1)} %copy-done.5, bf16[2048,896]{1,0:T(8,128)(2,1)} %collective-permute-done), kind=kOutput, calls=%fused_computation.17 | convolution fusion | flops 1879048192 | bytes 7602176 | tf_op jit(solution)/shard_map/dot_general | solution.py:112
  177.9 4.0 all-gather.7.cloned.1.call-done
  181.9 5.7 %add_convert_fusion.1 = bf16[1024,896]{1,0:T(8,128)(2,1)S(1)} fusion(f32[1024,896]{1,0:T(8,128)} %fusion.13, bf16[1024,1024]{1,0:T(8,128)(2,1)} %all-gather.7.cloned.1.call-done, bf16[2048,896]{1,0:T(8,128)(2,1)} %param.16), kind=kOutput, calls=%fused_computation.10 | convolution fusion | flops 1880883200 | bytes 9437184 | tf_op jit(solution)/shard_map/dot_general | solution.py:111
  187.7 3.8 add_convert_fusion
  191.5 0.3 pad_maximum_fusion
  191.8 2.1 copy.55
  194.0 40.1 %reduce-scatter.3.cloned.1.call-done = bf16[256,1792]{1,0:T(8,128)(2,1)} async-done(((bf16[1024,1792]{1,0:T(8,128)(2,1)}), bf16[256,1792]{1,0:T(8,128)(2,1)}) %reduce-scatter.3.cloned.1.call-update) | async-done | bytes 917520 | tf_op jit(solution)/shard_map/reduce_scatter | solution.py:116
  234.1 4.6 all-to-all-start
  239.1 22.5 %all-to-all-done = bf16[4,64,1792]{2,1,0:T(8,128)(2,1)S(1)} async-done(((bf16[4,64,1792]{2,1,0:T(8,128)(2,1)}), bf16[4,64,1792]{2,1,0:T(8,128)(2,1)S(1)}, u32[]{:S(2)}, u32[]{:S(2)}) %all-to-all-start) | async-done | bytes 917536 | tf_op jit(solution)/shard_map/all_to_all | solution.py:122
  261.9 1.4 copy.52
  263.3 2.7 reshape.177
  266.1 1.9 fusion.6
  268.0 0.4 convolution_convert_fusion.1
  268.4 11.2 %all_to_all.15 = bf16[4,8,7168]{2,1,0:T(8,128)(2,1)} all-to-all(bf16[4,8,7168]{2,1,0:T(8,128)(2,1)S(1)} %convolution_convert_fusion.1), channel_id=1, replica_groups=mesh['ctx'=8,'exp'=4] {'exp'}, dimensions={0} | all-to-all | bytes 917504 | tf_op jit(solution)/shard_map/all_to_all | solution.py:150
  279.9 64.8 %all-gather.11.cloned.1.call-done = bf16[256,7168]{1,0:T(8,128)(2,1)} async-done(((bf16[32,7168]{1,0:T(8,128)(2,1)}), bf16[256,7168]{1,0:T(8,128)(2,1)}) %all-gather.11.cloned.1.call-update) | async-done | bytes 3670032 | tf_op jit(solution)/shard_map/all_gather | solution.py:152
  344.7 4.3 fusion.3
  349.0 10.0 %convolution_convert_fusion = bf16[256,7168]{1,0:T(8,128)(2,1)} fusion(bf16[1,256,7168]{2,1,0:T(8,128)(2,1)} %param.23, bf16[256,7168]{1,0:T(8,128)(2,1)} %all-gather.11.cloned.1.call-done, bf16[1,7168,256]{2,1,0:T(8,128)(2,1)} %param.22, f32[256,256]{1,0:T(8,128)S(1)} %fusion.3), kind=kOutput, calls=%fused_computation.1 | convolution fusion | flops 1881276416 | bytes 14942208 | tf_op jit(solution)/shard_map/dot_general | solution.py:157
  359.1 79.5 %reduce-scatter.5.cloned.1.call-done = bf16[32,7168]{1,0:T(8,128)(2,1)} async-done(((bf16[256,7168]{1,0:T(8,128)(2,1)}), bf16[32,7168]{1,0:T(8,128)(2,1)}) %reduce-scatter.5.cloned.1.call-update) | async-done | bytes 458768 | tf_op jit(solution)/shard_map/reduce_scatter | solution.py:156
  438.6 3.5 all-to-all-start.2
  442.2 8.0 %all-to-all-done.2 = bf16[4,8,7168]{2,1,0:T(8,128)(2,1)S(1)} async-done(((bf16[4,8,7168]{2,1,0:T(8,128)(2,1)}), bf16[4,8,7168]{2,1,0:T(8,128)(2,1)S(1)}, u32[]{:S(2)}, u32[]{:S(2)}) %all-to-all-start.2) | async-done | bytes 458784 | tf_op jit(solution)/shard_map/all_to_all | solution.py:163
  450.1 2.1 fusion.5
  (48 shorter events, 1.7 us)
Async XLA Ops:
  7.2 59.4 %all-gather.5.cloned.1.call-start = ((), (), s32[]{:S(2)}) async-start(), calls=%async_computation.5 | async-start | bytes 2654208 | tf_op jit(solution)/shard_map/all_gather | solution.py:99
  7.9 127.2 %all-gather.9.cloned.1.call-start = ((), (), s32[]{:S(2)}) async-start(), calls=%async_computation.7 | async-start | bytes 2621440 | tf_op jit(solution)/shard_map/all_gather | solution.py:109
  90.8 91.1 %all-gather.7.cloned.1.call-start = ((), (), s32[]{:S(2)}) async-start(), calls=%async_computation.6 | async-start | bytes 2621440 | tf_op jit(solution)/shard_map/all_gather | solution.py:109
  90.9 81.4 %collective-permute-start = (bf16[2048,896]{1,0:T(8,128)(2,1)}, bf16[2048,896]{1,0:T(8,128)(2,1)}, u32[]{:S(2)}, u32[]{:S(2)}) collective-permute-start(bf16[2048,896]{1,0:T(8,128)(2,1)} %param.16), channel_id=1, source_target_pairs={{0,4},{4,0},{8,12},{12,8},{16,20},{20,16},{24,28},{28,24},{1,5},{5... | collective-permute-start | bytes 11010056 | tf_op jit(solution)/shard_map/ppermute | solution.py:104
  112.3 121.8 %reduce-scatter.3.cloned.1.call-start = ((), (), s32[]{:S(2)}) async-start(), calls=%async_computation.8 | async-start | bytes 4587520 | tf_op jit(solution)/shard_map/reduce_scatter | solution.py:116
  135.1 37.2 %copy-start.5 = (bf16[1024,1024]{1,0:T(8,128)(2,1)S(1)}, bf16[1024,1024]{1,0:T(8,128)(2,1)}, u32[]{:S(2)}) copy-start(bf16[1024,1024]{1,0:T(8,128)(2,1)} %all-gather.9.cloned.1.call-done) | copy-start | bytes 6291460
  181.9 5.7 %copy-start.6 = (bf16[1024,1024]{1,0:T(8,128)(2,1)S(1)}, bf16[1024,1024]{1,0:T(8,128)(2,1)}, u32[]{:S(2)}) copy-start(bf16[1024,1024]{1,0:T(8,128)(2,1)} %all-gather.7.cloned.1.call-done) | copy-start | bytes 6291460
  181.9 5.7 %copy-start.7 = (f32[1024,896]{1,0:T(8,128)S(1)}, f32[1024,896]{1,0:T(8,128)}, u32[]{:S(2)}) copy-start(f32[1024,896]{1,0:T(8,128)} %fusion.9) | copy-start | bytes 11010052
  194.0 44.7 %copy-start.4 = (bf16[7168]{0:T(1024)(128)(2,1)S(1)}, bf16[7168]{0:T(1024)(128)(2,1)}, u32[]{:S(2)}) copy-start(bf16[7168]{0:T(1024)(128)(2,1)} %param.18) | copy-start | bytes 43012
  194.0 44.7 %copy-start.3 = (s32[64,8]{0,1:T(8,128)S(1)}, s32[64,8]{0,1:T(8,128)}, u32[]{:S(2)}) copy-start(s32[64,8]{0,1:T(8,128)} %param.19) | copy-start | bytes 6148
  234.1 27.5 %all-to-all-start = ((bf16[4,64,1792]{2,1,0:T(8,128)(2,1)}), bf16[4,64,1792]{2,1,0:T(8,128)(2,1)S(1)}, u32[]{:S(2)}, u32[]{:S(2)}) async-start(bf16[4,64,1792]{2,1,0:T(8,128)(2,1)} %bitcast.50), calls=%async_computation.1 | async-start | bytes 1835008 | tf_op jit(solution)/shard_map/all_to_all | solution.py:122
  238.7 106.0 %all-gather.11.cloned.1.call-start = ((), (), s32[]{:S(2)}) async-start(), calls=%async_computation.9 | async-start | bytes 4128768 | tf_op jit(solution)/shard_map/all_gather | solution.py:152
  261.9 4.2 copy-start
  267.9 81.1 %copy-start.1 = (bf16[64,7168]{1,0:T(8,128)(2,1)}, bf16[64,7168]{1,0:T(8,128)(2,1)S(1)}, u32[]{:S(2)}) copy-start(bf16[64,7168]{1,0:T(8,128)(2,1)S(1)} %get-tuple-element.3) | copy-start | bytes 2752516
  279.6 158.9 %reduce-scatter.5.cloned.1.call-start = ((), (), s32[]{:S(2)}) async-start(), calls=%async_computation.10 | async-start | bytes 4128768 | tf_op jit(solution)/shard_map/reduce_scatter | solution.py:156
  359.1 83.0 %copy-start.2 = (f32[64,8]{0,1:T(8,128)S(1)}, f32[64,8]{0,1:T(8,128)}, u32[]{:S(2)}) copy-start(f32[64,8]{0,1:T(8,128)} %param.20) | copy-start | bytes 6148
  438.6 11.6 %all-to-all-start.2 = ((bf16[4,8,7168]{2,1,0:T(8,128)(2,1)}), bf16[4,8,7168]{2,1,0:T(8,128)(2,1)S(1)}, u32[]{:S(2)}, u32[]{:S(2)}) async-start(bf16[4,8,7168]{2,1,0:T(8,128)(2,1)} %bitcast.51), calls=%async_computation.4 | async-start | bytes 917504 | tf_op jit(solution)/shard_map/all_to_all | solution.py:163
Sparse Core Ops, SparseCore 0:
  10.0 56.4 all-gather.4
  90.9 44.0 all-gather.8
  137.2 44.6 all-gather.6
  194.1 39.9 reduce-scatter.2
  279.7 64.9 all-gather.10
  359.2 79.2 reduce-scatter.4

commit v4 on v3

--- a/solution.py
+++ b/solution.py
@@ -101,30 +101,40 @@
     ctx_count = lax.axis_size("ctx")
     levels = ctx_count // PAIR
     lines = [[level * PAIR + side for level in range(levels)] for side in range(PAIR)]
-    other = lax.ppermute(w_o, "ctx", [(c, c ^ 1) for c in range(ctx_count)])
+    swap = [(c, c ^ 1) for c in range(ctx_count)]
+    other = lax.ppermute(w_o, "ctx", swap)
     depth = w_o.shape[0] // HALVES
-    own_terms, other_terms = 0.0, 0.0
+    terms = [0.0, 0.0]
     for part in range(HALVES):
         heads = attention(queries, keys, query_place, key_place, w_uv, scale, part, HALVES)
         heads = lax.all_gather(heads, "ctx", axis=0, tiled=True, axis_index_groups=lines)
         rows = slice(part * depth, (part + 1) * depth)
-        own_terms += jnp.dot(heads, w_o[rows], preferred_element_type=jnp.float32)
-        other_terms += jnp.dot(heads, other[rows], preferred_element_type=jnp.float32)
-    terms = jnp.concatenate([own_terms, other_terms], axis=1).astype(jnp.bfloat16)
-    width = terms.shape[1]
-    terms = jnp.swapaxes(terms.reshape(levels, owner_count, token_count, width), 0, 1)
-    summed = lax.psum_scatter(
-        terms.reshape(owner_count * levels * token_count, width),
-        "exp",
-        scatter_dimension=0,
-        tiled=True,
-    ).reshape(levels, token_count, width)
-    spread = lax.all_to_all(
-        summed, "ctx", split_axis=0, concat_axis=0, tiled=True, axis_index_groups=lines
-    )
-    spread = jnp.swapaxes(spread, 0, 1).reshape(token_count, levels, PAIR, width // PAIR)
-    spread = jnp.where(lax.axis_index("ctx") % PAIR == 0, spread, spread[:, :, ::-1])
-    projected = spread.reshape(token_count, model_width).astype(jnp.float32)
+        for side, columns in enumerate((w_o, other)):
+            terms[side] += jnp.dot(heads, columns[rows], preferred_element_type=jnp.float32)
+    spread = []
+    for term in terms:
+        width = term.shape[1]
+        term = term.astype(jnp.bfloat16).reshape(levels, owner_count, token_count, width)
+        summed = lax.psum_scatter(
+            jnp.swapaxes(term, 0, 1).reshape(owner_count * levels * token_count, width),
+            "exp",
+            scatter_dimension=0,
+            tiled=True,
+        ).reshape(levels, token_count, width)
+        spread.append(
+            lax.all_to_all(
+                summed, "ctx", split_axis=0, concat_axis=0, tiled=True, axis_index_groups=lines
+            )
+        )
+    is_first = lax.axis_index("ctx") % PAIR == 0
+    projected = jnp.stack(
+        [jnp.where(is_first, *spread), jnp.where(is_first, *spread[::-1])], axis=1
+    )
+    projected = (
+        jnp.transpose(projected, (2, 0, 1, 3))
+        .reshape(token_count, model_width)
+        .astype(jnp.float32)
+    )
     attended = (residual.astype(jnp.float32) + projected).astype(jnp.bfloat16)
     level = attended.astype(jnp.float32)
     normed = (
@@ -153,12 +163,30 @@
     gate = jnp.dot(piece, w_gate[0], preferred_element_type=jnp.float32)
     lifted = jnp.dot(piece, w_up[0], preferred_element_type=jnp.float32)
     hidden = (jax.nn.silu(gate) * lifted).astype(jnp.bfloat16)
-    lowered = lax.psum_scatter(
-        jnp.dot(hidden, w_down[0], preferred_element_type=jnp.float32).astype(jnp.bfloat16),
-        "ctx",
-        scatter_dimension=0,
-        tiled=True,
-    )
+    slots = owner_count * capacity
+    hidden = hidden.reshape(levels, PAIR, slots, hidden.shape[1])
+    for_own = jnp.where(is_first, hidden[:, 0], hidden[:, 1]).reshape(levels * slots, -1)
+    for_other = jnp.where(is_first, hidden[:, 1], hidden[:, 0]).reshape(levels * slots, -1)
+    lowered = []
+    for part in range(HALVES):
+        span = model_width // HALVES
+        down = w_down[0][:, part * span : (part + 1) * span]
+        sent = lax.ppermute(
+            jnp.dot(for_other, down, preferred_element_type=jnp.float32).astype(jnp.bfloat16),
+            "ctx",
+            swap,
+        )
+        kept = jnp.dot(for_own, down, preferred_element_type=jnp.float32)
+        lowered.append(
+            lax.psum_scatter(
+                (kept + sent.astype(jnp.float32)).astype(jnp.bfloat16),
+                "ctx",
+                scatter_dimension=0,
+                tiled=True,
+                axis_index_groups=lines,
+            )
+        )
+    lowered = jnp.concatenate(lowered, axis=1)
     expert_out = lowered.reshape(owner_count, capacity, model_width)
     returned = lax.all_to_all(expert_out, "exp", split_axis=0, concat_axis=0, tiled=True)
     picked = jnp.einsum("toc,ocd->otd", select, returned, preferred_element_type=jnp.float32)

time: 460 us -> 455 us (0.989)
  waiting for transfers between devices: 330 us -> 320 us
  starting transfers between devices: 10.2 us -> 15.9 us
    reduce_scatter x2 -> x4, waiting for transfers between devices: 120 us -> 69.9 us  [the longest x2 43.7 us: per_device(): lax.psum_scatter(jnp.swapaxes(term, 0, 1).reshape(owner_count * levels *...]
    all_gather x2, waiting for transfers between devices: 26.5 us -> 63.3 us  [per_device(): lax.all_gather(heads, 'ctx', axis=0, tiled=True, axis_index_groups=lines)]
    ppermute x1 -> x3, waiting for transfers between devices: 30.6 us -> 43.1 us  [the longest x2 40.1 us: per_device(): lax.ppermute(jnp.dot(for_other, down, preferred_element_type=jnp.float32)...]
    all_to_all x1 -> x2, waiting for transfers between devices: 22.5 us -> 12.7 us  [per_device(): lax.all_to_all(summed, 'ctx', split_axis=0, concat_axis=0, tiled=True, ax...]
    dot_general x5 -> x9, matrix products: 31.8 us -> 27.6 us  [the longest x4 19.9 us: per_device(): jnp.dot(heads, columns[rows], preferred_element_type=jnp.float32)]
  transfers between devices with their start and end apart: 9 -> 14, of which waited for: 9 -> 12; matrix products, arithmetic and copies ran while one was open for 3% -> 7% of each run, Pallas kernels for 4% -> 4%
where the time goes in v4:
time: 455 us
  waiting for transfers between devices  320 us (70%)
  Pallas kernels  39.9 us (9%)
  matrix products  34.5 us (8%)
  starting transfers between devices  15.9 us (3%)
  between operations  14.4 us (3%)
  local copies, waits for them, and re-layouts  13.5 us (3%)
  blocking collectives  11.2 us (2%)
  other arithmetic  5.86 us (1%)
    all_gather x1, waiting for transfers between devices, per_device(): piece = lax.all_gather(flat_rows, 'ctx', axis=0, tiled=True)  65.1 us
    all_gather x2, waiting for transfers between devices, per_device(): lax.all_gather(heads, 'ctx', axis=0, tiled=True, axis_index_groups=lines)  63.3 us
    all_gather x1, waiting for transfers between devices, per_device(): keys = lax.all_gather(latent, 'ctx', axis=0, tiled=True)  56.8 us
    reduce_scatter x2, waiting for transfers between devices, per_device(): lax.psum_scatter(jnp.swapaxes(term, 0, 1).reshape(owner_count * levels *...  43.7 us
    ppermute x2, waiting for transfers between devices, per_device(): lax.ppermute(jnp.dot(for_other, down, preferred_element_type=jnp.float32)...  40.1 us
    pallas_call x2, Pallas kernels, attention(): pl.pallas_call(functools.partial(attend_heads, scale), grid=(head_count /...  39.9 us
    reduce_scatter x2, waiting for transfers between devices, per_device(): lax.psum_scatter((kept + sent.astype(jnp.float32)).astype(jnp.bfloat16),...  26.2 us
    dot_general x4, matrix products, per_device(): jnp.dot(heads, columns[rows], preferred_element_type=jnp.float32)  19.9 us
  transfers between devices with their start and end apart: 14, of which 12 were waited for; matrix products, arithmetic and copies ran while one was open for 7% of the time, Pallas kernels for 4%

profile of v4, /device:TPU:0, one launch (start us, length us, event | category | flops | bytes accessed | tf_op | source)
XLA Modules:
  0.0 454.8 jit_solution(16922594312318734690)
XLA Ops:
  9.7 56.8 %all-gather.5.cloned.1.call-done = bf16[2048,576]{0,1:T(8,128)(2,1)} async-done(((bf16[256,576]{0,1:T(8,128)(2,1)}), bf16[2048,576]{0,1:T(8,128)(2,1)}) %all-gather.5.cloned.1.call-update) | async-done | bytes 2359312 | tf_op jit(solution)/shard_map/all_gather | solution.py:99
  66.5 4.3 copy.41.keys_ref
  70.9 19.9 %shard_map.132 = bf16[256,1024]{1,0:T(8,128)(2,1)} custom-call(bf16[256,9216]{1,0:T(8,128)(2,1)} %query_ref.3, bf16[2048,576]{1,0:T(8,128)(2,1)} %copy.41.keys_ref, bf16[576,2048]{1,0:T(8,128)(2,1)} %bitcast.57, s32[256,1]{1,0:T(8,128)S(1)} %fusion.41.query_place_ref, s32[1,2048]{1,0:T(1,128)S(1)} %fusion.50.key_place_ref, bf16[16,512,128]{2,1,0:T(8,128)(2,1)} %w_uv_ref.3), custom_call_target="tpu_custom_call" | custom-call | flops 9126805504 | bytes 2883584 | tf_op jit(solution)/shard_map/pallas_call | solution.py:54
  90.9 20.0 %shard_map.131 = bf16[256,1024]{1,0:T(8,128)(2,1)} custom-call(bf16[256,9216]{1,0:T(8,128)(2,1)} %query_ref.3, bf16[2048,576]{1,0:T(8,128)(2,1)} %copy.41.keys_ref, bf16[576,2048]{1,0:T(8,128)(2,1)} %bitcast.58, s32[256,1]{1,0:T(8,128)S(1)} %fusion.41.query_place_ref, s32[1,2048]{1,0:T(1,128)S(1)} %fusion.50.key_place_ref, bf16[16,512,128]{2,1,0:T(8,128)(2,1)} %w_uv_ref.3), custom_call_target="tpu_custom_call" | custom-call | flops 9126805504 | bytes 2883584 | tf_op jit(solution)/shard_map/pallas_call | solution.py:54
  110.9 1.5 collective-permute-start
  112.4 22.7 %all-gather.9.cloned.1.call-done = bf16[1024,1024]{1,0:T(8,128)(2,1)} async-done(((bf16[256,1024]{1,0:T(8,128)(2,1)}), bf16[1024,1024]{1,0:T(8,128)(2,1)}) %all-gather.9.cloned.1.call-update) | async-done | bytes 2097168 | tf_op jit(solution)/shard_map/all_gather | solution.py:110
  135.1 6.3 %fusion.12 = f32[1024,896]{1,0:T(8,128)} fusion(bf16[1024,1024]{1,0:T(8,128)(2,1)} %all-gather.9.cloned.1.call-done, bf16[2048,896]{1,0:T(8,128)(2,1)} %param.16), kind=kOutput, calls=%fused_computation.24 | convolution fusion | flops 1879048192 | bytes 7602176 | tf_op jit(solution)/shard_map/dot_general | solution.py:113
  141.4 40.6 %all-gather.7.cloned.1.call-done = bf16[1024,1024]{1,0:T(8,128)(2,1)} async-done(((bf16[256,1024]{1,0:T(8,128)(2,1)}), bf16[1024,1024]{1,0:T(8,128)(2,1)}) %all-gather.7.cloned.1.call-update) | async-done | bytes 2097168 | tf_op jit(solution)/shard_map/all_gather | solution.py:110
  181.9 5.6 %add_convert_fusion.1 = bf16[1024,896]{1,0:T(8,128)(2,1)S(1)} fusion(f32[1024,896]{1,0:T(8,128)} %fusion.12, bf16[1024,1024]{1,0:T(8,128)(2,1)} %all-gather.7.cloned.1.call-done, bf16[2048,896]{1,0:T(8,128)(2,1)} %param.16), kind=kOutput, calls=%fused_computation.9 | convolution fusion | flops 1880883200 | bytes 9437184 | tf_op jit(solution)/shard_map/dot_general | solution.py:113
  187.5 1.4 copy.43
  189.2 3.0 collective-permute-done
  192.3 4.1 fusion.8
  196.4 3.9 add_convert_fusion
  201.8 15.9 %reduce-scatter.5.cloned.1.call-done = bf16[256,896]{1,0:T(8,128)(2,1)} async-done(((bf16[1024,896]{1,0:T(8,128)(2,1)}), bf16[256,896]{1,0:T(8,128)(2,1)}) %reduce-scatter.5.cloned.1.call-update) | async-done | bytes 458768 | tf_op jit(solution)/shard_map/reduce_scatter | solution.py:118
  217.7 4.6 %all-to-all-start = ((bf16[4,64,896]{2,1,0:T(8,128)(2,1)}), bf16[4,64,896]{2,1,0:T(8,128)(2,1)S(1)}, u32[]{:S(2)}, u32[]{:S(2)}) async-start(bf16[4,64,896]{2,1,0:T(8,128)(2,1)} %bitcast.67), calls=%async_computation.1 | async-start | bytes 917504 | tf_op jit(solution)/shard_map/all_to_all | solution.py:125
  222.3 27.8 %reduce-scatter.7.cloned.1.call-done = bf16[256,896]{1,0:T(8,128)(2,1)} async-done(((bf16[1024,896]{1,0:T(8,128)(2,1)}), bf16[256,896]{1,0:T(8,128)(2,1)}) %reduce-scatter.7.cloned.1.call-update) | async-done | bytes 458768 | tf_op jit(solution)/shard_map/reduce_scatter | solution.py:118
  250.1 4.6 %all-to-all-start.1 = ((bf16[4,64,896]{2,1,0:T(8,128)(2,1)}), bf16[4,64,896]{2,1,0:T(8,128)(2,1)S(1)}, u32[]{:S(2)}, u32[]{:S(2)}) async-start(bf16[4,64,896]{2,1,0:T(8,128)(2,1)} %bitcast.66), calls=%async_computation.3 | async-start | bytes 917504 | tf_op jit(solution)/shard_map/all_to_all | solution.py:125
  255.1 12.7 %all-to-all-done.1 = bf16[4,64,896]{2,1,0:T(8,128)(2,1)S(1)} async-done(((bf16[4,64,896]{2,1,0:T(8,128)(2,1)}), bf16[4,64,896]{2,1,0:T(8,128)(2,1)S(1)}, u32[]{:S(2)}, u32[]{:S(2)}) %all-to-all-start.1) | async-done | bytes 458784 | tf_op jit(solution)/shard_map/all_to_all | solution.py:125
  269.4 2.7 reshape.198
  272.2 1.9 fusion.5
  274.5 11.2 %all_to_all.20 = bf16[4,8,7168]{2,1,0:T(8,128)(2,1)} all-to-all(bf16[4,8,7168]{2,1,0:T(8,128)(2,1)S(1)} %convolution_convert_fusion), channel_id=1, replica_groups=mesh['ctx'=8,'exp'=4] {'exp'}, dimensions={0} | all-to-all | bytes 917504 | tf_op jit(solution)/shard_map/all_to_all | solution.py:160
  285.8 65.1 %all-gather.11.cloned.1.call-done = bf16[256,7168]{1,0:T(8,128)(2,1)} async-done(((bf16[32,7168]{1,0:T(8,128)(2,1)}), bf16[256,7168]{1,0:T(8,128)(2,1)}) %all-gather.11.cloned.1.call-update) | async-done | bytes 3670032 | tf_op jit(solution)/shard_map/all_gather | solution.py:162
  350.9 4.4 fusion.2
  359.3 20.5 %collective-permute-done.2 = bf16[128,3584]{1,0:T(8,128)(2,1)S(1)} collective-permute-done((bf16[128,3584]{1,0:T(8,128)(2,1)S(1)}, bf16[128,3584]{1,0:T(8,128)(2,1)S(1)}, u32[]{:S(2)}, u32[]{:S(2)}) %collective-permute-start.2) | collective-permute-done | bytes 917536 | tf_op jit(solution)/shard_map/ppermute | solution.py:174
  381.2 1.9 convolution_convert_fusion.2
  383.8 19.6 %collective-permute-done.1 = bf16[128,3584]{1,0:T(8,128)(2,1)S(1)} collective-permute-done((bf16[128,3584]{1,0:T(8,128)(2,1)S(1)}, bf16[128,3584]{1,0:T(8,128)(2,1)S(1)}, u32[]{:S(2)}, u32[]{:S(2)}) %collective-permute-start.1) | collective-permute-done | bytes 917536 | tf_op jit(solution)/shard_map/ppermute | solution.py:174
  403.4 2.9 add_convert_fusion.3
  406.3 26.1 %reduce-scatter.9.cloned.1.call-done = bf16[32,3584]{1,0:T(8,128)(2,1)} async-done(((bf16[128,3584]{1,0:T(8,128)(2,1)}), bf16[32,3584]{1,0:T(8,128)(2,1)}) %reduce-scatter.9.cloned.1.call-update) | async-done | bytes 229392 | tf_op jit(solution)/shard_map/reduce_scatter | solution.py:181
  432.4 1.8 maximum_bitcast_fusion
  434.3 3.5 all-to-all-start.3
  437.9 8.0 %all-to-all-done.3 = bf16[4,8,7168]{2,1,0:T(8,128)(2,1)S(1)} async-done(((bf16[4,8,7168]{2,1,0:T(8,128)(2,1)}), bf16[4,8,7168]{2,1,0:T(8,128)(2,1)S(1)}, u32[]{:S(2)}, u32[]{:S(2)}) %all-to-all-start.3) | async-done | bytes 458784 | tf_op jit(solution)/shard_map/all_to_all | solution.py:191
  445.9 2.1 fusion.4
  (70 shorter events, 13.0 us)
Async XLA Ops:
  7.2 59.4 %all-gather.5.cloned.1.call-start = ((), (), s32[]{:S(2)}) async-start(), calls=%async_computation.8 | async-start | bytes 2654208 | tf_op jit(solution)/shard_map/all_gather | solution.py:99
  7.9 127.2 %all-gather.9.cloned.1.call-start = ((), (), s32[]{:S(2)}) async-start(), calls=%async_computation.10 | async-start | bytes 2621440 | tf_op jit(solution)/shard_map/all_gather | solution.py:110
  90.8 91.1 %all-gather.7.cloned.1.call-start = ((), (), s32[]{:S(2)}) async-start(), calls=%async_computation.9 | async-start | bytes 2621440 | tf_op jit(solution)/shard_map/all_gather | solution.py:110
  110.9 106.9 %reduce-scatter.5.cloned.1.call-start = ((), (), s32[]{:S(2)}) async-start(), calls=%async_computation.11 | async-start | bytes 2293760 | tf_op jit(solution)/shard_map/reduce_scatter | solution.py:118
  110.9 81.4 %collective-permute-start = (bf16[2048,896]{1,0:T(8,128)(2,1)}, bf16[2048,896]{1,0:T(8,128)(2,1)}, u32[]{:S(2)}, u32[]{:S(2)}) collective-permute-start(bf16[2048,896]{1,0:T(8,128)(2,1)} %param.16), channel_id=1, source_target_pairs={{0,4},{4,0},{8,12},{12,8},{16,20},{20,16},{24,28},{28,24},{1,5},{5... | collective-permute-start | bytes 11010056 | tf_op jit(solution)/shard_map/ppermute | solution.py:105
  187.5 4.8 %copy-start.8 = (bf16[1024,1024]{1,0:T(8,128)(2,1)S(1)}, bf16[1024,1024]{1,0:T(8,128)(2,1)}, u32[]{:S(2)}) copy-start(bf16[1024,1024]{1,0:T(8,128)(2,1)} %all-gather.9.cloned.1.call-done) | copy-start | bytes 6291460
  189.0 61.1 %reduce-scatter.7.cloned.1.call-start = ((), (), s32[]{:S(2)}) async-start(), calls=%async_computation.12 | async-start | bytes 2293760 | tf_op jit(solution)/shard_map/reduce_scatter | solution.py:118
  189.2 7.2 %copy-start.9 = (bf16[1024,1024]{1,0:T(8,128)(2,1)S(1)}, bf16[1024,1024]{1,0:T(8,128)(2,1)}, u32[]{:S(2)}) copy-start(bf16[1024,1024]{1,0:T(8,128)(2,1)} %all-gather.7.cloned.1.call-done) | copy-start | bytes 6291460
  201.8 52.9 %copy-start.5 = (bf16[7168]{0:T(1024)(128)(2,1)S(1)}, bf16[7168]{0:T(1024)(128)(2,1)}, u32[]{:S(2)}) copy-start(bf16[7168]{0:T(1024)(128)(2,1)} %param.18) | copy-start | bytes 43012
  201.8 53.0 %copy-start.4 = (s32[64,8]{0,1:T(8,128)S(1)}, s32[64,8]{0,1:T(8,128)}, u32[]{:S(2)}) copy-start(s32[64,8]{0,1:T(8,128)} %param.19) | copy-start | bytes 6148
  217.7 32.4 %all-to-all-start = ((bf16[4,64,896]{2,1,0:T(8,128)(2,1)}), bf16[4,64,896]{2,1,0:T(8,128)(2,1)S(1)}, u32[]{:S(2)}, u32[]{:S(2)}) async-start(bf16[4,64,896]{2,1,0:T(8,128)(2,1)} %bitcast.67), calls=%async_computation.1 | async-start | bytes 917504 | tf_op jit(solution)/shard_map/all_to_all | solution.py:125
  250.1 17.7 %all-to-all-start.1 = ((bf16[4,64,896]{2,1,0:T(8,128)(2,1)}), bf16[4,64,896]{2,1,0:T(8,128)(2,1)S(1)}, u32[]{:S(2)}, u32[]{:S(2)}) async-start(bf16[4,64,896]{2,1,0:T(8,128)(2,1)} %bitcast.66), calls=%async_computation.3 | async-start | bytes 917504 | tf_op jit(solution)/shard_map/all_to_all | solution.py:125
  254.7 96.2 %all-gather.11.cloned.1.call-start = ((), (), s32[]{:S(2)}) async-start(), calls=%async_computation.13 | async-start | bytes 4128768 | tf_op jit(solution)/shard_map/all_gather | solution.py:162
  269.4 2.7 copy-start.1
  274.1 81.2 %copy-start.2 = (bf16[64,7168]{1,0:T(8,128)(2,1)}, bf16[64,7168]{1,0:T(8,128)(2,1)S(1)}, u32[]{:S(2)}) copy-start(bf16[64,7168]{1,0:T(8,128)(2,1)S(1)} %get-tuple-element.3) | copy-start | bytes 2752516
  285.7 120.5 %reduce-scatter.11.cloned.1.call-start = ((), (), s32[]{:S(2)}) async-start(), calls=%async_computation.15 | async-start | bytes 1146880 | tf_op jit(solution)/shard_map/reduce_scatter | solution.py:181
  350.9 4.4 copy-start.6
  350.9 5.3 %copy-start.7 = (bf16[256,7168]{1,0:T(8,128)(2,1)S(1)}, bf16[256,7168]{1,0:T(8,128)(2,1)}, u32[]{:S(2)}) copy-start(bf16[256,7168]{1,0:T(8,128)(2,1)} %all-gather.11.cloned.1.call-done) | copy-start | bytes 11010052
  356.2 2.0 copy-start
  358.6 21.1 %collective-permute-start.2 = (bf16[128,3584]{1,0:T(8,128)(2,1)S(1)}, bf16[128,3584]{1,0:T(8,128)(2,1)S(1)}, u32[]{:S(2)}, u32[]{:S(2)}) collective-permute-start(bf16[128,3584]{1,0:T(8,128)(2,1)S(1)} %convolution_convert_fusion.1), channel_id=1, source_target_pairs={{0,4},{4,0},{8,12},{12,8},{16,20},{20,16},{24,28},{28,24},{1,5},{5... | collective-permute-start | bytes 2752520 | tf_op jit(solution)/shard_map/ppermute | solution.py:174
  381.2 51.3 %reduce-scatter.9.cloned.1.call-start = ((), (), s32[]{:S(2)}) async-start(), calls=%async_computation.14 | async-start | bytes 1146880 | tf_op jit(solution)/shard_map/reduce_scatter | solution.py:181
  383.2 20.2 %collective-permute-start.1 = (bf16[128,3584]{1,0:T(8,128)(2,1)S(1)}, bf16[128,3584]{1,0:T(8,128)(2,1)S(1)}, u32[]{:S(2)}, u32[]{:S(2)}) collective-permute-start(bf16[128,3584]{1,0:T(8,128)(2,1)S(1)} %convolution_convert_fusion.2), channel_id=1, source_target_pairs={{0,4},{4,0},{8,12},{12,8},{16,20},{20,16},{24,28},{28,24},{1,5},{5... | collective-permute-start | bytes 2752520 | tf_op jit(solution)/shard_map/ppermute | solution.py:174
  406.2 31.5 %copy-start.3 = (f32[64,8]{0,1:T(8,128)S(1)}, f32[64,8]{0,1:T(8,128)}, u32[]{:S(2)}) copy-start(f32[64,8]{0,1:T(8,128)} %param.20) | copy-start | bytes 6148
  434.3 11.6 %all-to-all-start.3 = ((bf16[4,8,7168]{2,1,0:T(8,128)(2,1)}), bf16[4,8,7168]{2,1,0:T(8,128)(2,1)S(1)}, u32[]{:S(2)}, u32[]{:S(2)}) async-start(bf16[4,8,7168]{2,1,0:T(8,128)(2,1)} %maximum_bitcast_fusion), calls=%async_computation.7 | async-start | bytes 917504 | tf_op jit(solution)/shard_map/all_to_all | solution.py:191
Sparse Core Ops, SparseCore 0:
  10.0 56.4 all-gather.4
  90.9 44.1 all-gather.8
  137.3 44.6 all-gather.6
  189.1 28.5 reduce-scatter.4
  220.3 29.8 reduce-scatter.6
  285.9 64.9 all-gather.10
  381.3 24.7 reduce-scatter.10
  408.4 24.0 reduce-scatter.8
